TPU v7x, 32 devices: a whole 2x2x4 slice. The times are simulated.
32 devices in a mesh: grp: 2 (over y), tile: 4 (over z), var: 4 (over x, core).
Axes of the slice: x: 2, y: 2, z: 4, core: 2. Of those that a mesh axis runs over, the one named last changes fastest.
Arguments:
- control: float32 [8, 128, 2048], P('var', ('grp', 'tile')), parts along dimension 1, may hold values from -6 to 6
- diffusivity: float32 [2, 128, 2048], P(None, ('grp', 'tile')), parts along dimension 1, may hold values from 0.05 to 0.95
- land_mask: int32 [128, 2048], P(('grp', 'tile')), parts along dimension 0, may hold values 0 or 1
- panel_tile: int32 [1024, 1], P(('grp', 'tile')), parts along dimension 0, may hold values from 0 to 3; in each aligned block of 128 rows (0 to 127, 128 to 255, ...) at most 64 rows name the same one
- panel_row: int32 [1024], P(('grp', 'tile')), parts along dimension 0, may hold values from 0 to 15
- panel_cols: int32 [1024, 128], P(('grp', 'tile')), parts along dimension 0, may hold values from 0 to 2047
- obs_values: float32 [1024, 128], P(('grp', 'tile')), parts along dimension 0, may hold values from -6 to 6
- obs_weights: float32 [1024, 128], P(('grp', 'tile')), parts along dimension 0, may hold values from 0.5 to 4
- panel_sensor: int32 [1024], P(('grp', 'tile')), parts along dimension 0, may hold values from 0 to 1
- sensitivity: float32 [2, 8], replicated, may hold values from 0.2 to 1
- cross_factor: float32 [8, 8], replicated, may hold values from -0.45 to 2
Outputs:
- gradient: float32 [8, 128, 2048], P('var', ('grp', 'tile')), parts along dimension 1
There are 2 independent parts, one for each index of `grp`. A program takes and returns all parts, laid end to end along the dimension named above; an argument that names none is the same for every part. Nothing has to cross between parts.
Inputs may be any that keep to these rules, and one draw needn't show every extreme that they name: `panel_tile`: among the 128 panels held by one tile index, at most 64 name the same tile.
All inputs are finite; a program needn't handle non-finite values. No bound on the sum of `land_mask` on one device may be relied on, other than what follows from the above.
Results may differ from a plain program's by a relative error of at most 0.00014.
Values sent between devices are 32-bit elements; how exact they have to be, the bound alone decides.
No kernel may reach another device: no remote copies, remote signals or barrier semaphores. Data moves between devices by JAX's collectives and lax.ppermute only.
A program may use at most 128 MiB of HBM per device.

v0:
```python
import jax
import jax.numpy as jnp
from jax import lax
from jax.sharding import PartitionSpec as P

PASSES = 10


def with_halo(cells, sides, width):
    for axis, dim in sides:
        count = lax.axis_size(axis)
        ends = count - 1
        head = lax.slice_in_dim(cells, 0, width, axis=dim)
        tail = lax.slice_in_dim(cells, cells.shape[dim] - width, cells.shape[dim], axis=dim)
        cells = jnp.concatenate(
            [
                lax.ppermute(tail, axis, [(i, (i + 1) % count) for i in range(ends)]),
                cells,
                lax.ppermute(head, axis, [((i + 1) % count, i) for i in range(ends)]),
            ],
            axis=dim,
        )
    return cells


def one_pass(values, row_kappa, col_kappa):
    row_pad = jnp.pad(row_kappa, ((1, 1), (0, 0)))
    col_pad = jnp.pad(col_kappa, ((0, 0), (1, 1)))
    face_up = 0.125 * (row_kappa + row_pad[:-2])
    face_down = 0.125 * (row_kappa + row_pad[2:])
    face_left = 0.125 * (col_kappa + col_pad[:, :-2])
    face_right = 0.125 * (col_kappa + col_pad[:, 2:])
    vals_rows = jnp.pad(values, ((0, 0), (1, 1), (0, 0)))
    vals_cols = jnp.pad(values, ((0, 0), (0, 0), (1, 1)))
    return (
        values
        - face_up * (values - vals_rows[:, :-2])
        - face_down * (values - vals_rows[:, 2:])
        - face_left * (values - vals_cols[:, :, :-2])
        - face_right * (values - vals_cols[:, :, 2:])
    )


def diffuse(values, coef_wide):
    margin = PASSES
    rows_dev = values.shape[1]
    row_k = coef_wide[0, margin - 1 : margin + rows_dev + 1]
    col_k = coef_wide[1, margin - 1 : margin + rows_dev + 1]

    def advance(index, current):
        padded = with_halo(current, (("tile", 1),), 1)
        return one_pass(padded, row_k, col_k)[:, 1:-1]

    return lax.fori_loop(0, PASSES, advance, values)


def local(
    control,
    diffusivity,
    land_mask,
    panel_tile,
    panel_row,
    panel_cols,
    obs_values,
    obs_weights,
    panel_sensor,
    sensitivity,
    cross_factor,
):
    highest = lax.Precision.HIGHEST
    var_dev, rows_dev, width_cols = control.shape
    tiles = lax.axis_size("tile")
    var_pos = lax.axis_index("var")
    margin = PASSES
    coef_wide = with_halo(diffusivity, (("tile", 1),), margin)
    smooth = diffuse(control, coef_wide)
    own_rows = lax.dynamic_slice_in_dim(cross_factor, var_pos * var_dev, var_dev, 0)
    factor = own_rows
    state = jnp.einsum(
        "uv,vrc->urc", factor, lax.all_gather(smooth, "var", axis=0, tiled=True), precision=highest
    )
    panels_dev = panel_tile.shape[0]
    slots = 2 * panels_dev // tiles
    total_slots = tiles * slots
    target = panel_tile[:, 0]
    hits = (target[:, None] == jnp.arange(tiles, dtype=jnp.int32)[None, :]).astype(jnp.float32)
    panel_ids = jnp.arange(panels_dev, dtype=jnp.int32)
    lower = (panel_ids[:, None] > panel_ids[None, :]).astype(jnp.float32)
    before = jnp.dot(lower, hits, precision=highest)
    rank_in = jnp.sum(before * hits, axis=1).astype(jnp.int32)
    slot_pos = target * slots + rank_in
    slot_hot = (jnp.arange(total_slots, dtype=jnp.int32)[:, None] == slot_pos[None, :]).astype(
        jnp.float32
    )
    sensor_hot = (
        panel_sensor[:, None] == jnp.arange(sensitivity.shape[0], dtype=jnp.int32)[None, :]
    ).astype(jnp.float32)
    panel_sens = jnp.dot(sensor_hot, sensitivity, precision=highest)
    observed = jnp.stack([obs_values, obs_weights], axis=1)
    cell_ids = (panel_row[:, None] * width_cols + panel_cols).astype(jnp.float32)
    panel_width = panel_cols.shape[1]
    send_obs = jnp.einsum("tp,pkw->tkw", slot_hot, observed, precision=highest)
    send_sens = jnp.dot(slot_hot, panel_sens, precision=highest)
    send_cells = jnp.dot(slot_hot, cell_ids, precision=highest).astype(jnp.int32)
    got_obs, got_sens = (
        lax.all_to_all(
            send_obs.reshape(tiles, slots, 2, panel_width),
            "tile",
            split_axis=0,
            concat_axis=0,
            tiled=True,
        ),
        lax.all_to_all(
            send_sens.reshape(tiles, slots, -1), "tile", split_axis=0, concat_axis=0, tiled=True
        ),
    )
    got_cells = lax.all_to_all(
        send_cells.reshape(tiles, slots, panel_width),
        "tile",
        split_axis=0,
        concat_axis=0,
        tiled=True,
    )
    got_obs = got_obs.reshape(total_slots, 2, panel_width)
    got_sens = got_sens.reshape(total_slots, -1)
    got_cells = got_cells.reshape(total_slots, panel_width)
    own_sens = lax.dynamic_slice_in_dim(got_sens, var_pos * var_dev, var_dev, 1)
    fields = jnp.concatenate([state, land_mask.astype(jnp.float32)[None]], axis=0)
    flat_fields = fields.reshape(var_dev + 1, rows_dev * width_cols)
    picked_all = flat_fields[:, got_cells]
    picked = picked_all[:var_dev]
    usable = picked_all[var_dev]
    partial_obs = jnp.sum(own_sens.T[:, :, None] * picked, axis=0)
    model_obs = lax.psum(partial_obs, "var")
    misfit = got_obs[:, 1] * usable * (model_obs - got_obs[:, 0])
    spread = own_sens.T[:, :, None] * misfit[None]
    adjoint = jnp.zeros((var_dev, rows_dev * width_cols), jnp.float32)
    adjoint = adjoint.at[:, got_cells.reshape(-1)].add(spread.reshape(var_dev, -1))
    adjoint = adjoint.reshape(var_dev, rows_dev, width_cols)
    factor = own_rows
    pulled = lax.psum_scatter(
        jnp.einsum("uv,urc->vrc", factor, adjoint, precision=highest),
        "var",
        scatter_dimension=0,
        tiled=True,
    )
    return control + diffuse(pulled, coef_wide)


def solution(mesh):
    return jax.shard_map(
        local,
        mesh=mesh,
        in_specs=(
            P("var", ("grp", "tile"), None),
            P(None, ("grp", "tile"), None),
            P(("grp", "tile"), None),
            P(("grp", "tile"), None),
            P(("grp", "tile")),
            P(("grp", "tile"), None),
            P(("grp", "tile"), None),
            P(("grp", "tile"), None),
            P(("grp", "tile")),
            P(),
            P(),
        ),
        out_specs=P("var", ("grp", "tile"), None),
        check_vma=False,
    )
```

profile of v0, /device:TPU:0, one launch (start us, length us, event | category | flops | bytes accessed | tf_op | source)
XLA Modules:
  0.0 682.2 jit_solution(9507205363941595819)
XLA Ops:
  7.6 4.9 collective-permute-start.4
  17.4 5.9 all-to-all-start.1
  25.4 81.9 %while.24 = (s32[]{:T(128)}, f32[2,16,2048]{2,1,0:T(8,128)S(1)}, f32[18,2048]{1,0:T(8,128)S(1)}, f32[18,2048]{1,0:T(8,128)S(1)}, s32[]{:T(128)}) while((s32[]{:T(128)}, f32[2,16,2048]{2,1,0:T(8,128)S(1)}, f32[18,2048]{1,0:T(8,128)S(1)}, f32[18,2048]{1,0:T(8,128)S(1)}, s32[]{:T(128)}) %tuple.81), condition=%wide.region_2.3_spmd, body=%wide.region_1.2_spmd.sunk | while | flops 1228802 | bytes 6291597 | solution.py:54
  26.8 4.6 collective-permute-start.1
  34.8 4.8 collective-permute-start.1
  43.0 4.8 collective-permute-start.1
  51.2 4.8 collective-permute-start.1
  59.4 4.8 collective-permute-start.1
  67.6 4.8 collective-permute-start.1
  75.8 4.8 collective-permute-start.1
  84.0 4.8 collective-permute-start.1
  92.2 4.8 collective-permute-start.1
  100.4 4.8 collective-permute-start.1
  109.0 6.5 all-to-all-start
  130.7 8.6 %copy.47 = f32[3,32768]{0,1:T(8,128)} copy(f32[3,32768]{1,0:T(4,128)S(1)} %pad_maximum_fusion.2) | data formatting | bytes 786432 | tf_op jit(solution)/shard_map/concatenate | solution.py:128
  139.2 114.7 %gather_fusion = f32[32768,3]{1,0:T(8,128)} fusion(f32[3,32768]{0,1:T(8,128)} %copy.47, s32[32768]{0:T(1024)S(1)} %fusion.33), kind=kCustom, calls=%fused_computation | custom fusion | bytes 917504 | tf_op jit(solution)/shard_map/gather | solution.py:130
  254.0 9.7 %copy.48 = f32[256,128,3]{1,0,2:T(8,128)S(1)} copy(f32[256,128,3]{2,1,0:T(8,128)} %bitcast.77) | data formatting | bytes 786432 | tf_op jit(solution)/shard_map/gather | solution.py:130
  264.7 31.3 %all-reduce.10.cloned.1.call-done = f32[256,128]{1,0:T(8,128)} async-done(((f32[256,128]{1,0:T(8,128)}), f32[256,128]{1,0:T(8,128)}) %all-reduce.10.cloned.1.call-update) | async-done | bytes 131088 | tf_op jit(solution)/shard_map/psum | solution.py:134
  297.2 8.3 %copy.49 = f32[32768,2]{1,0:T(8,128)} copy(f32[32768,2]{0,1:T(2,128)S(1)} %fusion.29) | data formatting | bytes 524288 | tf_op jit(solution)/shard_map/mul | solution.py:136
  305.6 218.3 %scatter_custom_fusion = f32[2,32768]{0,1:T(8,128)} fusion(s32[32768]{0:T(1024)S(1)} %bitcast.85, f32[32768,2]{1,0:T(8,128)} %copy.49, f32[]{:T(128)} %constant.59.clone.1), kind=kCustom, calls=%fused_computation.52 | custom fusion | flops 65536 | bytes 262656 | tf_op jit(solution)/shard_map/scatter-add | solution.py:138
  523.8 17.7 %fusion.53 = f32[8,16,2048]{2,0,1:T(8,128)S(1)} fusion(f32[2,16,2048]{0,2,1:T(8,128)} %bitcast.76, f32[8,8]{1,0:T(8,128)S(1)} %copy-done, s32[]{:T(128)S(6)} %select_n.24), kind=kOutput, calls=%fused_computation.100 | convolution fusion | flops 6291456 | bytes 1311748 | tf_op jit(solution)/shard_map/uv,urc->vrc/dot_general | solution.py:142
  543.2 23.0 %reduce-scatter.2.cloned.1.call-done = f32[2,16,2048]{2,1,0:T(8,128)} async-done(((f32[8,16,2048]{2,1,0:T(8,128)}), f32[2,16,2048]{2,1,0:T(8,128)}) %reduce-scatter.2.cloned.1.call-update) | async-done | bytes 262160 | tf_op jit(solution)/shard_map/reduce_scatter | solution.py:141
  566.2 107.8 %while.25 = (s32[]{:T(128)}, f32[2,16,2048]{2,1,0:T(8,128)}, f32[18,2048]{1,0:T(8,128)S(1)}, f32[18,2048]{1,0:T(8,128)S(1)}, s32[]{:T(128)}) while((s32[]{:T(128)}, f32[2,16,2048]{2,1,0:T(8,128)}, f32[18,2048]{1,0:T(8,128)S(1)}, f32[18,2048]{1,0:T(8,128)S(1)}, s32[]{:T(128)}) %tuple.94), condition=%wide.region_8.9_spmd, body=%wide.region_7.8_spmd.sunk | while | flops 1228802 | bytes 6291597 | solution.py:54
  579.0 4.8 collective-permute-start.3
  589.8 4.8 collective-permute-start.3
  600.6 4.8 collective-permute-start.3
  611.4 4.8 collective-permute-start.3
  622.2 4.8 collective-permute-start.3
  633.0 4.8 collective-permute-start.3
  643.8 4.8 collective-permute-start.3
  654.6 4.8 collective-permute-start.3
  665.4 4.8 collective-permute-start.3
  (300 shorter events, 126.8 us)
Async XLA Ops:
  7.6 16.6 %collective-permute-start.4 = (f32[2,10,2048]{2,1,0:T(8,128)S(1)}, f32[2,10,2048]{2,1,0:T(8,128)S(1)}, u32[]{:S(2)}, u32[]{:S(2)}) collective-permute-start(f32[2,10,2048]{2,1,0:T(8,128)S(1)} %get-tuple-element.163), channel_id=1, source_target_pairs={{0,4},{4,8},{8,12},{1,5},{5,9},{9,13},{2,6},{6,10},{10,14},{3,7},{... | collective-permute-start | bytes 491528 | tf_op jit(solution)/shard_map/ppermute | solution.py:17
  12.6 11.7 %collective-permute-start.5 = (f32[2,10,2048]{2,1,0:T(8,128)S(1)}, f32[2,10,2048]{2,1,0:T(8,128)S(1)}, u32[]{:S(2)}, u32[]{:S(2)}) collective-permute-start(f32[2,10,2048]{2,1,0:T(8,128)S(1)} %get-tuple-element.164), channel_id=1, source_target_pairs={{4,0},{8,4},{12,8},{5,1},{9,5},{13,9},{6,2},{10,6},{14,10},{7,3},{... | collective-permute-start | bytes 491528 | tf_op jit(solution)/shard_map/ppermute | solution.py:19
  17.4 91.6 %all-to-all-start.1 = ((f32[4,1,512]{2,1,0:T(1,128)}), f32[4,1,512]{2,1,0:T(1,128)S(1)}, u32[]{:S(2)}, u32[]{:S(2)}) async-start(f32[4,1,512]{2,1,0:T(1,128)} %reshape.135), calls=%async_computation.1 | async-start | bytes 16384 | tf_op jit(solution)/shard_map/all_to_all | solution.py:113
  23.3 104.4 %all-gather.2.cloned.1.call-start = ((), (), s32[]{:S(2)}) async-start(), calls=%async_computation.4 | async-start | bytes 1310720 | tf_op jit(solution)/shard_map/all_gather | solution.py:80
  25.4 6.3 collective-permute-start
  33.5 6.4 collective-permute-start
  34.8 6.3 collective-permute-start.1
  41.7 6.4 collective-permute-start
  43.0 6.3 collective-permute-start.1
  49.9 6.4 collective-permute-start
  51.2 6.3 collective-permute-start.1
  58.1 6.4 collective-permute-start
  59.4 6.3 collective-permute-start.1
  66.3 6.4 collective-permute-start
  67.6 6.3 collective-permute-start.1
  74.5 6.4 collective-permute-start
  82.7 6.4 collective-permute-start
  90.9 6.4 collective-permute-start
  99.1 6.4 collective-permute-start
  109.0 12.4 %all-to-all-start = ((s32[4,64,128]{2,1,0:T(8,128)}), s32[4,64,128]{2,1,0:T(8,128)S(1)}, u32[]{:S(2)}, u32[]{:S(2)}) async-start(s32[4,64,128]{2,1,0:T(8,128)} %bitcast.2), calls=%async_computation | async-start | bytes 262144 | tf_op jit(solution)/shard_map/all_to_all | solution.py:117
  121.4 143.3 %all-to-all-start.2 = ((f32[4,64,2,128]{3,1,2,0:T(8,128)}), f32[4,64,2,128]{3,1,2,0:T(8,128)S(1)}, u32[]{:S(2)}, u32[]{:S(2)}) async-start(f32[4,64,2,128]{3,1,2,0:T(8,128)} %copy.44), calls=%async_computation.2 | async-start | bytes 524288 | tf_op jit(solution)/shard_map/all_to_all | solution.py:106
  124.8 171.2 %all-reduce.10.cloned.1.call-start = ((), (), s32[]{:S(2)}) async-start(), calls=%async_computation.5 | async-start | bytes 262144 | tf_op jit(solution)/shard_map/psum | solution.py:134
  264.5 301.7 %reduce-scatter.2.cloned.1.call-start = ((), (), s32[]{:S(2)}) async-start(), calls=%async_computation.6 | async-start | bytes 1310720 | tf_op jit(solution)/shard_map/reduce_scatter | solution.py:141
  577.7 6.4 collective-permute-start.2
  588.5 6.4 collective-permute-start.2
  599.3 6.4 collective-permute-start.2
  610.1 6.4 collective-permute-start.2
  620.9 6.4 collective-permute-start.2
  631.7 6.4 collective-permute-start.2
  642.5 6.4 collective-permute-start.2
  653.3 6.4 collective-permute-start.2
  664.1 6.4 collective-permute-start.2
  (23 other events, 674.8 us)
Sparse Core Ops, SparseCore 0:
  108.1 19.5 all-gather.1
  264.6 31.3 all-reduce.9
  543.3 22.8 reduce-scatter.1
where the time goes:
time: 687 us; the launch traced here: 682 us
  other arithmetic  251 us (37%)
  local copies, waits for them, and re-layouts  165 us (24%)
  starting transfers between devices  144 us (21%)
  waiting for transfers between devices  83.6 us (12%)
  matrix products  23.5 us (3%)
  between operations  13.3 us (2%)
    scatter-add x1, other arithmetic, local(): adjoint.at[:, got_cells.reshape(-1)].add(spread.reshape(var_dev, -1))  218 us
    gather x2, local copies, waits for them, and re-layouts, local(): picked_all = flat_fields[:, got_cells]  124 us
    ppermute x21, starting transfers between devices, with_halo(): lax.ppermute(tail, axis, [(i, (i + 1) % count) for i in range(ends)])  101 us
    psum x1, waiting for transfers between devices, local(): model_obs = lax.psum(partial_obs, 'var')  31.3 us
    ppermute x21, starting transfers between devices, with_halo(): lax.ppermute(head, axis, [((i + 1) % count, i) for i in range(ends)])  27.3 us
    reduce_scatter x1, waiting for transfers between devices, local(): lax.psum_scatter(jnp.einsum('uv,urc->vrc', factor, adjoint, precision=hig...  23 us
    ppermute x21, waiting for transfers between devices, with_halo(): lax.ppermute(tail, axis, [(i, (i + 1) % count) for i in range(ends)])  22.9 us
    dot_general x1, matrix products, local(): jnp.einsum('uv,urc->vrc', factor, adjoint, precision=highest)  17.7 us
  transfers between devices with their start and end apart: 48, of which 24 were waited for; matrix products, arithmetic and copies ran while one was open for 23% of the time, Pallas kernels for 0%

commit v1 on v0

v1 whole, which is shorter than its diff:
```python
import functools

import jax
import jax.numpy as jnp
from jax import lax
from jax.experimental import pallas as pl
from jax.experimental.pallas import tpu as pltpu
from jax.sharding import PartitionSpec as P

PASSES = 10
LANES = 128
GROUP = 8
VMEM = pl.BlockSpec(memory_space=pltpu.VMEM)
SMEM = pl.BlockSpec(memory_space=pltpu.SMEM)
F32 = jnp.float32


def call(body, outs, ins, scratch=(), limit=16, cost=None):
    return pl.pallas_call(
        body,
        out_shape=outs,
        in_specs=ins,
        out_specs=[VMEM] * len(outs),
        scratch_shapes=list(scratch),
        compiler_params=pltpu.CompilerParams(vmem_limit_bytes=limit << 20),
        cost_estimate=cost,
    )


def cost(cycles):
    return pl.CostEstimate(flops=cycles * 4096, bytes_accessed=cycles * 1024, transcendentals=0)


def response(sens_ref, factor_ref, sensor, variable):
    total = sens_ref[sensor, 0] * factor_ref[0, variable]
    for u in range(1, factor_ref.shape[0]):
        total = total + sens_ref[sensor, u] * factor_ref[u, variable]
    return total


def combine_kernel(pos_ref, sens_ref, factor_ref, control_ref, own_ref, other_ref):
    var_dev = control_ref.shape[0]
    pos = pos_ref[0]
    core = pos % 2
    for sensor, out_ref in ((1 - core, other_ref), (core, own_ref)):
        total = None
        for v in range(var_dev):
            term = response(sens_ref, factor_ref, sensor, pos * var_dev + v) * control_ref[v]
            total = term if total is None else total + term
        out_ref[...] = total


def pack_kernel(slots, pos_ref, tile_ref, row_ref, sensor_ref, value_ref, weight_ref, cols_ref,
                send_ref, cells_ref, count_ref):
    tiles = send_ref.shape[0]
    panels, width = value_ref.shape
    core = pos_ref[0] % 2
    cells_ref[...] = cols_ref[...].astype(F32)
    send_ref[...] = jnp.zeros(send_ref.shape, F32)
    for t in range(tiles):
        count_ref[t] = 0
    pad_tiles = -(-tiles // 8) * 8
    sub = lax.broadcasted_iota(jnp.int32, (pad_tiles, LANES), 0)
    lane = lax.broadcasted_iota(jnp.int32, (pad_tiles, LANES), 1)

    def place(p, meta):
        t = tile_ref[p]
        keep = sensor_ref[p] == core
        slot = count_ref[t]
        count_ref[t] = slot + keep.astype(jnp.int32)
        trash = 3 * slots + 7
        for part, ref in enumerate((value_ref, weight_ref, cells_ref)):
            at = jnp.where(keep, part * slots + slot, trash)
            send_ref[t, pl.ds(at, 1), :] = ref[pl.ds(p, 1), :]
        where = jnp.where(keep, slot, LANES)
        return jnp.where((sub == t) & (lane == where), row_ref[p].astype(F32), meta)

    meta = lax.fori_loop(0, panels, place, jnp.zeros((pad_tiles, LANES), F32), unroll=4)
    for t in range(tiles):
        meta = jnp.where((sub == t) & (lane == slots), count_ref[t].astype(F32), meta)
    for t in range(tiles):
        send_ref[t, pl.ds(3 * slots, 1), :] = meta[t : t + 1]


def pieces(values):
    top = values.astype(jnp.bfloat16).astype(F32)
    return top, values - top


def scatter_kernel(slots, got_ref, meta_ref, weight_out, value_out, acc_ref):
    tiles = got_ref.shape[0]
    rows, width_cols = weight_out.shape
    blocks = width_cols // LANES
    acc_ref[...] = jnp.zeros(acc_ref.shape, F32)
    block_ids = lax.broadcasted_iota(jnp.int32, (blocks, LANES), 0)
    lane_ids = lax.broadcasted_iota(jnp.int32, (LANES, LANES), 0)
    sub = lax.broadcasted_iota(jnp.int32, (GROUP, LANES), 0)

    def source(s, carry):
        count = meta_ref[s, slots]

        def group(g, carry):
            base = pl.multiple_of(g * GROUP, GROUP)
            value = got_ref[s, pl.ds(base, GROUP), :]
            weight = got_ref[s, pl.ds(slots + base, GROUP), :]
            cell = got_ref[s, pl.ds(2 * slots + base, GROUP), :].astype(jnp.int32)
            weight = jnp.where(sub + base < count, weight, 0.0)
            parts = pieces(weight) + pieces(weight * value)
            low = cell % LANES
            high = cell // LANES
            for k in range(GROUP):
                in_block = block_ids == high[k : k + 1]
                left = jnp.concatenate(
                    [jnp.where(in_block, parts[i][k : k + 1], 0.0) for i in (0, 2, 1, 3)], axis=0
                ).astype(jnp.bfloat16)
                right = jnp.where(lane_ids == low[k : k + 1], 1.0, 0.0).astype(jnp.bfloat16)
                both = lax.dot_general(
                    left, right, (((1,), (1,)), ((), ())), preferred_element_type=F32
                )
                row = meta_ref[s, base + k]
                at = pl.ds(pl.multiple_of(row * 2 * blocks, 2 * blocks), 2 * blocks)
                acc_ref[at, :] += both[: 2 * blocks] + both[2 * blocks :]
            return carry

        return lax.fori_loop(0, (count + GROUP - 1) // GROUP, group, carry)

    lax.fori_loop(0, tiles, source, 0)
    for b in range(blocks):
        at = slice(b * LANES, (b + 1) * LANES)
        weight_out[:, at] = acc_ref[pl.ds(b, rows, stride=2 * blocks), :]
        value_out[:, at] = acc_ref[pl.ds(blocks + b, rows, stride=2 * blocks), :]


def edges_kernel(first_ref, second_ref, kappa_ref, total_ref, head_ref, tail_ref):
    rows = first_ref.shape[0]
    margin = head_ref.shape[1]
    total_ref[...] = first_ref[...] + second_ref[...]
    head_ref[0] = total_ref[:margin]
    tail_ref[0] = total_ref[rows - margin :]
    for i in range(2):
        head_ref[1 + i] = kappa_ref[i, :margin]
        tail_ref[1 + i] = kappa_ref[i, rows - margin :]


def ring_rows(rows, margin):
    return -(-(rows + 2 * margin) // 8) * 8


def lay_ring(ref, own, below, above):
    rows, margin, total = own.shape[0], below.shape[0], ref.shape[0]
    ref[rows:total] = jnp.zeros((total - rows, ref.shape[1]), F32)
    ref[:rows] = own
    ref[rows : rows + margin] = below
    ref[total - margin :] = above


def block(ref, j):
    return ref[:, j * LANES : (j + 1) * LANES]


def sideways(ref, j, blocks):
    here = block(ref, j)
    shape = here.shape
    lane = lax.broadcasted_iota(jnp.int32, shape, 1)
    left = pltpu.roll(here, 1, 1)
    right = pltpu.roll(here, LANES - 1, 1)
    before = pltpu.roll(block(ref, j - 1), 1, 1) if j else jnp.zeros(shape, F32)
    after = pltpu.roll(block(ref, j + 1), LANES - 1, 1) if j + 1 < blocks else jnp.zeros(shape, F32)
    return jnp.where(lane == 0, before, left), jnp.where(lane == LANES - 1, after, right)


def face_weights(coef_ref, row_ref, col_ref, rows, margin, has_above, has_below):
    total, width = row_ref.shape
    blocks = width // LANES
    r = lax.broadcasted_iota(jnp.int32, (total, LANES), 0)
    inside = (
        (r < rows)
        | ((r < rows + margin) & has_below)
        | ((r >= total - margin) & has_above)
    )
    scale = jnp.where(inside, 0.125, 0.0)
    unit = jnp.where(inside, 1.0, 0.0)
    for j in range(blocks):
        at = slice(j * LANES, (j + 1) * LANES)
        k_row, k_col = block(row_ref, j), block(col_ref, j)
        k_left, k_right = sideways(col_ref, j, blocks)
        up = scale * (k_row + pltpu.roll(k_row, 1, 0))
        down = scale * (k_row + pltpu.roll(k_row, total - 1, 0))
        left = scale * (k_col + k_left)
        right = scale * (k_col + k_right)
        coef_ref[0, :, at] = unit - up - down - left - right
        coef_ref[1, :, at] = up
        coef_ref[2, :, at] = down
        coef_ref[3, :, at] = left
        coef_ref[4, :, at] = right


def one_pass(source_ref, target_ref, coef_ref):
    total, width = source_ref.shape
    blocks = width // LANES
    for j in range(blocks):
        at = slice(j * LANES, (j + 1) * LANES)
        here = source_ref[:, at]
        left, right = sideways(source_ref, j, blocks)
        target_ref[:, at] = (
            coef_ref[0, :, at] * here
            + coef_ref[1, :, at] * pltpu.roll(here, 1, 0)
            + coef_ref[2, :, at] * pltpu.roll(here, total - 1, 0)
            + coef_ref[3, :, at] * left
            + coef_ref[4, :, at] * right
        )


def diffuse(one_ref, two_ref, coef_ref):
    def twice(index, carry):
        one_pass(one_ref, two_ref, coef_ref)
        one_pass(two_ref, one_ref, coef_ref)
        return carry

    lax.fori_loop(0, PASSES // 2, twice, 0)


def analyse_kernel(tiles, pos_ref, own_ref, above_ref, below_ref, kappa_ref, mask_ref, weight_ref,
                   value_ref, coef_ref, adjoint_ref, head_ref, tail_ref, one_ref, two_ref):
    rows, margin = own_ref.shape[0], above_ref.shape[1]
    lay_ring(one_ref, kappa_ref[0], below_ref[1], above_ref[1])
    lay_ring(two_ref, kappa_ref[1], below_ref[2], above_ref[2])
    tile = pos_ref[1]
    face_weights(coef_ref, one_ref, two_ref, rows, margin, tile > 0, tile + 1 < tiles)
    lay_ring(one_ref, own_ref[...], below_ref[0], above_ref[0])
    diffuse(one_ref, two_ref, coef_ref)
    adjoint_ref[...] = mask_ref[...].astype(F32) * (
        weight_ref[...] * one_ref[:rows] - value_ref[...]
    )
    head_ref[...] = adjoint_ref[:margin]
    tail_ref[...] = adjoint_ref[rows - margin :]


def spread_kernel(own_ref, above_ref, below_ref, coef_ref, out_ref, one_ref, two_ref):
    lay_ring(one_ref, own_ref[...], below_ref[...], above_ref[...])
    diffuse(one_ref, two_ref, coef_ref)
    out_ref[...] = one_ref[: out_ref.shape[0]]


def result_kernel(pos_ref, sens_ref, factor_ref, control_ref, own_ref, other_ref, out_ref):
    var_dev = control_ref.shape[0]
    pos = pos_ref[0]
    core = pos % 2
    for v in range(var_dev):
        mine = response(sens_ref, factor_ref, core, pos * var_dev + v)
        theirs = response(sens_ref, factor_ref, 1 - core, pos * var_dev + v)
        out_ref[v] = control_ref[v] + mine * own_ref[...] + theirs * other_ref[...]


def swap(values, axis, bit):
    count = lax.axis_size(axis)
    return lax.ppermute(values, axis, [(i, i ^ bit) for i in range(count)])


def neighbours(head, tail):
    count = lax.axis_size("tile")
    above = lax.ppermute(tail, "tile", [(i, i + 1) for i in range(count - 1)])
    below = lax.ppermute(head, "tile", [(i + 1, i) for i in range(count - 1)])
    return above, below


def local(control, diffusivity, land_mask, panel_tile, panel_row, panel_cols, obs_values,
          obs_weights, panel_sensor, sensitivity, cross_factor):
    var_dev, rows, width = control.shape
    tiles, members = lax.axis_size("tile"), lax.axis_size("var")
    panels, panel_width = panel_cols.shape
    slots = 2 * panels // tiles
    blocks = width // LANES
    margin = PASSES
    total = ring_rows(rows, margin)
    field = jax.ShapeDtypeStruct((rows, width), F32)
    edge = jax.ShapeDtypeStruct((margin, width), F32)
    edge3 = jax.ShapeDtypeStruct((3, margin, width), F32)
    pos = jnp.stack([lax.axis_index("var"), lax.axis_index("tile")]).astype(jnp.int32)

    own, other = call(combine_kernel, [field, field], [SMEM] * 3 + [VMEM], cost=cost(1000))(
        pos, sensitivity, cross_factor, control
    )
    (send,) = call(
        functools.partial(pack_kernel, slots),
        [jax.ShapeDtypeStruct((tiles, 3 * slots + 8, panel_width), F32)],
        [SMEM] * 4 + [VMEM] * 3,
        [pltpu.VMEM((panels, panel_width), F32), pltpu.SMEM((tiles,), jnp.int32)],
        cost=cost(3000),
    )(pos, panel_tile.reshape(-1), panel_row, panel_sensor, obs_values, obs_weights, panel_cols)
    got = lax.all_to_all(send, "tile", split_axis=0, concat_axis=0, tiled=True)

    part = own + swap(other, "var", 1)
    bit = 2
    while 2 * bit < members:
        part = part + swap(part, "var", bit)
        bit *= 2
    smooth_in, head, tail = call(
        edges_kernel, [field, edge3, edge3], [VMEM] * 3, cost=cost(1000)
    )(part, swap(part, "var", bit), diffusivity)
    above, below = neighbours(head, tail)

    weight_sum, value_sum = call(
        functools.partial(scatter_kernel, slots),
        [field, field],
        [VMEM, SMEM],
        [pltpu.VMEM((rows * 2 * blocks, LANES), F32)],
        cost=cost(10000),
    )(got, got[:, 3 * slots].astype(jnp.int32))

    ring = pltpu.VMEM((total, width), F32)
    coef, adjoint, head, tail = call(
        functools.partial(analyse_kernel, tiles),
        [jax.ShapeDtypeStruct((5, total, width), F32), field, edge, edge],
        [SMEM] + [VMEM] * 7,
        [ring, ring],
        cost=cost(5000),
    )(pos, smooth_in, above, below, diffusivity, land_mask, weight_sum, value_sum)
    above, below = neighbours(head, tail)
    (mine,) = call(spread_kernel, [field], [VMEM] * 4, [ring, ring], cost=cost(4000))(
        adjoint, above, below, coef
    )
    (out,) = call(
        result_kernel,
        [jax.ShapeDtypeStruct(control.shape, F32)],
        [SMEM] * 3 + [VMEM] * 3,
        cost=cost(1000),
    )(pos, sensitivity, cross_factor, control, mine, swap(mine, "var", 1))
    return out


def solution(mesh):
    return jax.shard_map(
        local,
        mesh=mesh,
        in_specs=(
            P("var", ("grp", "tile"), None),
            P(None, ("grp", "tile"), None),
            P(("grp", "tile"), None),
            P(("grp", "tile"), None),
            P(("grp", "tile")),
            P(("grp", "tile"), None),
            P(("grp", "tile"), None),
            P(("grp", "tile"), None),
            P(("grp", "tile")),
            P(),
            P(),
        ),
        out_specs=P("var", ("grp", "tile"), None),
        check_vma=False,
    )
```

time: 687 us -> 62 us (0.09)
  other arithmetic: 251 us -> 0.09 us
  local copies, waits for them, and re-layouts: 165 us -> 6.88 us
  starting transfers between devices: 144 us -> 17.9 us
  waiting for transfers between devices: 83.6 us -> 20.7 us
  matrix products: 23.5 us -> 0 us
  Pallas kernels: 0 us -> 15.8 us
  between operations: 13.3 us -> 0.13 us
    scatter-add x1 -> x0, other arithmetic: 218 us -> none  [local(): adjoint.at[:, got_cells.reshape(-1)].add(spread.reshape(var_dev, -1))]
    gather x2 -> x0, local copies, waits for them, and re-layouts: 124 us -> none  [local(): picked_all = flat_fields[:, got_cells]]
    ppermute x42 -> x7, starting transfers between devices: 128 us -> 11.6 us  [the longest x2 7.31 us: neighbours(): above = lax.ppermute(tail, 'tile', [(i, i + 1) for i in range(count - 1)])]
    psum x1 -> x0, waiting for transfers between devices: 31.3 us -> none  [local(): model_obs = lax.psum(partial_obs, 'var')]
    dot_general x7 -> x0, matrix products: 23.5 us -> none  [the longest x1 17.7 us: local(): jnp.einsum('uv,urc->vrc', factor, adjoint, precision=highest)]
    reduce_scatter x1 -> x0, waiting for transfers between devices: 23 us -> none  [local(): lax.psum_scatter(jnp.einsum('uv,urc->vrc', factor, adjoint, precision=hig...]
    slice x121 -> x1, local copies, waits for them, and re-layouts: 18.2 us -> 0.01 us  [local(): got[:, 3 * slots].astype(jnp.int32)]
    pallas_call x0 -> x7, Pallas kernels: none -> 15.8 us  [the longest x1 4.79 us: local(): call(functools.partial(analyse_kernel, tiles), [jax.ShapeDtypeStruct((5,...]
  transfers between devices with their start and end apart: 48 -> 8, of which waited for: 24 -> 7; matrix products, arithmetic and copies ran while one was open for 23% -> 0% of each run, Pallas kernels for 0% -> 5%
where the time goes in v1:
time: 62 us; the launch traced here: 61.5 us
  waiting for transfers between devices  20.7 us (33%)
  starting transfers between devices  17.9 us (29%)
  Pallas kernels  15.8 us (25%)
  local copies, waits for them, and re-layouts  6.88 us (11%)
    ppermute x2, waiting for transfers between devices, neighbours(): below = lax.ppermute(head, 'tile', [(i + 1, i) for i in range(count - 1)])  8.5 us
    ppermute x2, starting transfers between devices, neighbours(): above = lax.ppermute(tail, 'tile', [(i, i + 1) for i in range(count - 1)])  7.31 us
    unnamed x28, local copies, waits for them, and re-layouts  6.88 us
    ppermute x3, waiting for transfers between devices, swap(): return lax.ppermute(values, axis, [(i, i ^ bit) for i in range(count)])  6.73 us
    all_to_all x1, starting transfers between devices, local(): got = lax.all_to_all(send, 'tile', split_axis=0, concat_axis=0, tiled=True)  6.32 us
    ppermute x2, waiting for transfers between devices, neighbours(): above = lax.ppermute(tail, 'tile', [(i, i + 1) for i in range(count - 1)])  5.44 us
    pallas_call x1, Pallas kernels, local(): call(functools.partial(analyse_kernel, tiles), [jax.ShapeDtypeStruct((5,...  4.79 us
    pallas_call x1, Pallas kernels, local(): call(spread_kernel, [field], [VMEM] * 4, [ring, ring], cost=cost(4000))  4.22 us
  transfers between devices with their start and end apart: 8, of which 7 were waited for; matrix products, arithmetic and copies ran while one was open for 0% of the time, Pallas kernels for 5%

profile of v1, /device:TPU:0, one launch (start us, length us, event | category | flops | bytes accessed | tf_op | source)
XLA Modules:
  0.0 61.5 jit_solution(14065860867243631522)
XLA Ops:
  0.0 0.1 pad_add_fusion.pos_ref
  0.1 0.9 %copy-done.4 = f32[128,128]{1,0:T(8,128)S(1)} copy-done((f32[128,128]{1,0:T(8,128)S(1)}, f32[128,128]{1,0:T(8,128)}, u32[]{:S(2)}) %copy-start.4) | copy-done | bytes 65560
  1.0 0.8 %copy-done.5 = f32[128,128]{1,0:T(8,128)S(1)} copy-done((f32[128,128]{1,0:T(8,128)S(1)}, f32[128,128]{1,0:T(8,128)}, u32[]{:S(2)}) %copy-start.5) | copy-done | bytes 65560
  1.8 0.8 %copy-done.6 = s32[128,128]{1,0:T(8,128)S(1)} copy-done((s32[128,128]{1,0:T(8,128)S(1)}, s32[128,128]{1,0:T(8,128)}, u32[]{:S(2)}) %copy-start.6) | copy-done | bytes 65560
  2.7 0.7 %copy-done.11 = s32[128,1]{0,1:T(1,128)S(1)} copy-done((s32[128,1]{0,1:T(1,128)S(1)}, s32[128,1]{0,1:T(1,128)}, u32[]{:S(2)}) %copy-start.11) | copy-done | bytes 536
  3.3 0.7 %copy-done.12 = s32[128]{0:T(128)S(1)} copy-done((s32[128]{0:T(128)S(1)}, s32[128]{0:T(128)}, u32[]{:S(2)}) %copy-start.12) | copy-done | bytes 536
  4.0 0.7 %copy-done.13 = s32[128]{0:T(128)S(1)} copy-done((s32[128]{0:T(128)S(1)}, s32[128]{0:T(128)}, u32[]{:S(2)}) %copy-start.13) | copy-done | bytes 536
  4.6 2.4 %shard_map.111 = f32[4,200,128]{2,1,0:T(8,128)} custom-call(s32[2]{0:T(128)S(1)} %pad_add_fusion.pos_ref, s32[128]{0:T(128)S(1)} %bitcast.6, s32[128]{0:T(128)S(1)} %copy-done.12, s32[128]{0:T(128)S(1)} %copy-done.13, f32[128,128]{1,0:T(8,128)S(1)} %copy-done.4, f32[128,128]{1,0:T(8,128)S(1)} %copy-done.5, s32[128,128]{1,0:T(8,128)S(1)} %copy-done.6), custom_call_target="tpu_custom_call" | custom-call | flops 12288000 | bytes 3072000 | tf_op jit(solution)/shard_map/pallas_call | solution.py:284
  7.1 6.3 %all-to-all-start = ((f32[4,200,128]{2,1,0:T(8,128)}), f32[4,200,128]{2,1,0:T(8,128)S(1)}, u32[]{:S(2)}, u32[]{:S(2)}) async-start(f32[4,200,128]{2,1,0:T(8,128)} %shard_map.111), calls=%async_computation | async-start | bytes 819200 | tf_op jit(solution)/shard_map/all_to_all | solution.py:291
  13.4 0.9 %copy-done = f32[2,16,2048]{2,1,0:T(8,128)S(1)} copy-done((f32[2,16,2048]{2,1,0:T(8,128)S(1)}, f32[2,16,2048]{2,1,0:T(8,128)}, u32[]{:S(2)}) %copy-start) | copy-done | bytes 262168
  14.3 0.7 %copy-done.7 = f32[8,8]{1,0:T(8,128)S(1)} copy-done((f32[8,8]{1,0:T(8,128)S(1)}, f32[8,8]{1,0:T(8,128)}, u32[]{:S(2)}) %copy-start.7) | copy-done | bytes 280
  15.0 0.7 %copy-done.9 = f32[2,8]{1,0:T(2,128)S(1)} copy-done((f32[2,8]{1,0:T(2,128)S(1)}, f32[2,8]{1,0:T(2,128)}, u32[]{:S(2)}) %copy-start.9) | copy-done | bytes 88
  15.7 0.7 %shard_map.109 = (f32[16,2048]{1,0:T(8,128)S(1)}, f32[16,2048]{1,0:T(8,128)S(1)}) custom-call(s32[2]{0:T(128)S(1)} %pad_add_fusion.pos_ref, f32[2,8]{1,0:T(2,128)S(1)} %copy-done.9, f32[8,8]{1,0:T(8,128)S(1)} %copy-done.7, f32[2,16,2048]{2,1,0:T(8,128)S(1)} %copy-done), custom_call_target="tpu_custom_call" | custom-call | flops 4096000 | bytes 1024000 | tf_op jit(solution)/shard_map/pallas_call | solution.py:281
  16.4 0.1 collective-permute-start
  16.5 1.3 %collective-permute-done = f32[16,2048]{1,0:T(8,128)S(1)} collective-permute-done((f32[16,2048]{1,0:T(8,128)S(1)}, f32[16,2048]{1,0:T(8,128)S(1)}, u32[]{:S(2)}, u32[]{:S(2)}) %collective-permute-start) | collective-permute-done | bytes 131104 | tf_op jit(solution)/shard_map/ppermute | solution.py:257
  17.8 1.6 %collective-permute-start.1 = (f32[16,2048]{1,0:T(8,128)S(1)}, f32[16,2048]{1,0:T(8,128)S(1)}, u32[]{:S(2)}, u32[]{:S(2)}) collective-permute-start(f32[16,2048]{1,0:T(8,128)S(1)} %add.3.first_ref), channel_id=1, source_target_pairs={{0,2},{1,3},{2,0},{3,1},{4,6},{5,7},{6,4},{7,5},{8,10},{9,11},{10,... | collective-permute-start | bytes 393224 | tf_op jit(solution)/shard_map/ppermute | solution.py:257
  19.4 4.1 %collective-permute-done.1.second_ref = f32[16,2048]{1,0:T(8,128)S(1)} collective-permute-done((f32[16,2048]{1,0:T(8,128)S(1)}, f32[16,2048]{1,0:T(8,128)S(1)}, u32[]{:S(2)}, u32[]{:S(2)}) %collective-permute-start.1) | collective-permute-done | bytes 131104 | tf_op jit(solution)/shard_map/ppermute | solution.py:257
  23.5 0.1 shard_map.110
  23.5 4.0 %collective-permute-start.2 = (f32[3,10,2048]{2,1,0:T(8,128)S(1)}, f32[3,10,2048]{2,1,0:T(8,128)S(1)}, u32[]{:S(2)}, u32[]{:S(2)}) collective-permute-start(f32[3,10,2048]{2,1,0:T(8,128)S(1)} %get-tuple-element.19), channel_id=1, source_target_pairs={{0,4},{4,8},{8,12},{1,5},{5,9},{9,13},{2,6},{6,10},{10,14},{3,7},{... | collective-permute-start | bytes 737288 | tf_op jit(solution)/shard_map/ppermute | solution.py:262
  27.5 1.3 %collective-permute-start.3 = (f32[3,10,2048]{2,1,0:T(8,128)S(1)}, f32[3,10,2048]{2,1,0:T(8,128)S(1)}, u32[]{:S(2)}, u32[]{:S(2)}) collective-permute-start(f32[3,10,2048]{2,1,0:T(8,128)S(1)} %get-tuple-element.20), channel_id=1, source_target_pairs={{4,0},{8,4},{12,8},{5,1},{9,5},{13,9},{6,2},{10,6},{14,10},{7,3},{... | collective-permute-start | bytes 737288 | tf_op jit(solution)/shard_map/ppermute | solution.py:263
  28.8 2.2 %shard_map.112 = (f32[16,2048]{1,0:T(8,128)S(1)}, f32[16,2048]{1,0:T(8,128)S(1)}) custom-call(f32[4,200,128]{2,1,0:T(8,128)S(1)} %all-to-all-done.got_ref, s32[4,128]{1,0:T(4,128)S(1)} %convert_bitcast_fusion.meta_ref), custom_call_target="tpu_custom_call" | custom-call | flops 40960000 | bytes 10240000 | tf_op jit(solution)/shard_map/pallas_call | solution.py:303
  31.1 4.2 %collective-permute-done.2.above_ref = f32[3,10,2048]{2,1,0:T(8,128)S(1)} collective-permute-done((f32[3,10,2048]{2,1,0:T(8,128)S(1)}, f32[3,10,2048]{2,1,0:T(8,128)S(1)}, u32[]{:S(2)}, u32[]{:S(2)}) %collective-permute-start.2) | collective-permute-done | bytes 245792 | tf_op jit(solution)/shard_map/ppermute | solution.py:262
  35.3 4.1 %collective-permute-done.3.below_ref = f32[3,10,2048]{2,1,0:T(8,128)S(1)} collective-permute-done((f32[3,10,2048]{2,1,0:T(8,128)S(1)}, f32[3,10,2048]{2,1,0:T(8,128)S(1)}, u32[]{:S(2)}, u32[]{:S(2)}) %collective-permute-start.3) | collective-permute-done | bytes 245792 | tf_op jit(solution)/shard_map/ppermute | solution.py:263
  39.5 4.8 %shard_map.113 = (f32[5,40,2048]{2,1,0:T(8,128)S(1)}, f32[16,2048]{1,0:T(8,128)S(1)}, f32[10,2048]{1,0:T(8,128)S(1)}, f32[10,2048]{1,0:T(8,128)S(1)}) custom-call(s32[2]{0:T(128)S(1)} %pad_add_fusion.pos_ref, f32[16,2048]{1,0:T(8,128)S(1)} %get-tuple-element.18.own_ref, f32[3,10,2048]{2,1,0:T(8,128)S(1)} %collective-permute-done.2.above_ref, ...), custom_call_target="tpu_custom_call" | custom-call | flops 20480000 | bytes 5120000 | tf_op jit(solution)/shard_map/pallas_call | solution.py:312
  44.3 3.4 %collective-permute-start.4 = (f32[10,2048]{1,0:T(8,128)S(1)}, f32[10,2048]{1,0:T(8,128)S(1)}, u32[]{:S(2)}, u32[]{:S(2)}) collective-permute-start(f32[10,2048]{1,0:T(8,128)S(1)} %get-tuple-element.24), channel_id=1, source_target_pairs={{0,4},{4,8},{8,12},{1,5},{5,9},{9,13},{2,6},{6,10},{10,14},{3,7},{... | collective-permute-start | bytes 245768 | tf_op jit(solution)/shard_map/ppermute | solution.py:262
  47.6 1.3 %collective-permute-start.5 = (f32[10,2048]{1,0:T(8,128)S(1)}, f32[10,2048]{1,0:T(8,128)S(1)}, u32[]{:S(2)}, u32[]{:S(2)}) collective-permute-start(f32[10,2048]{1,0:T(8,128)S(1)} %get-tuple-element.25), channel_id=1, source_target_pairs={{4,0},{8,4},{12,8},{5,1},{9,5},{13,9},{6,2},{10,6},{14,10},{7,3},{... | collective-permute-start | bytes 245768 | tf_op jit(solution)/shard_map/ppermute | solution.py:263
  48.9 1.2 %collective-permute-done.4.above_ref = f32[10,2048]{1,0:T(8,128)S(1)} collective-permute-done((f32[10,2048]{1,0:T(8,128)S(1)}, f32[10,2048]{1,0:T(8,128)S(1)}, u32[]{:S(2)}, u32[]{:S(2)}) %collective-permute-start.4) | collective-permute-done | bytes 81952 | tf_op jit(solution)/shard_map/ppermute | solution.py:262
  50.1 4.4 %collective-permute-done.5.below_ref = f32[10,2048]{1,0:T(8,128)S(1)} collective-permute-done((f32[10,2048]{1,0:T(8,128)S(1)}, f32[10,2048]{1,0:T(8,128)S(1)}, u32[]{:S(2)}, u32[]{:S(2)}) %collective-permute-start.5) | collective-permute-done | bytes 81952 | tf_op jit(solution)/shard_map/ppermute | solution.py:263
  54.5 4.2 %shard_map.114.own_ref = f32[16,2048]{1,0:T(8,128)S(1)} custom-call(f32[16,2048]{1,0:T(8,128)S(1)} %get-tuple-element.23.own_ref, f32[10,2048]{1,0:T(8,128)S(1)} %collective-permute-done.4.above_ref, f32[10,2048]{1,0:T(8,128)S(1)} %collective-permute-done.5.below_ref, f32[5,40,2048]{2,1,0:T(8,128)S(1)} %get-tuple-element.26.coef_ref), custom_call_target="tpu_custom_call" | custom-call | flops 16384000 | bytes 4096000 | tf_op jit(solution)/shard_map/pallas_call | solution.py:320
  58.7 0.1 collective-permute-start.6
  58.8 1.3 %collective-permute-done.6.other_ref = f32[16,2048]{1,0:T(8,128)S(1)} collective-permute-done((f32[16,2048]{1,0:T(8,128)S(1)}, f32[16,2048]{1,0:T(8,128)S(1)}, u32[]{:S(2)}, u32[]{:S(2)}) %collective-permute-start.6) | collective-permute-done | bytes 131104 | tf_op jit(solution)/shard_map/ppermute | solution.py:257
  60.1 1.4 %shard_map.115 = f32[2,16,2048]{2,1,0:T(8,128)} custom-call(s32[2]{0:T(128)S(1)} %pad_add_fusion.pos_ref, f32[2,8]{1,0:T(2,128)S(1)} %copy-done.10, f32[8,8]{1,0:T(8,128)S(1)} %copy-done.8, f32[2,16,2048]{2,1,0:T(8,128)S(1)} %copy-done.1, f32[16,2048]{1,0:T(8,128)S(1)} %shard_map.114.own_ref, f32[16,2048]{1,0:T(8,128)S(1)} %collective-permute-done.6.other_ref), custom_call_target="tpu_custom_call" | custom-call | flops 4096000 | bytes 1024000 | tf_op jit(solution)/shard_map/pallas_call | solution.py:323
  (23 shorter events, 0.1 us)
Async XLA Ops:
  0.0 23.5 %copy-start.2 = (f32[2,16,2048]{2,1,0:T(8,128)S(1)}, f32[2,16,2048]{2,1,0:T(8,128)}, u32[]{:S(2)}) copy-start(f32[2,16,2048]{2,1,0:T(8,128)} %kappa_ref.3) | copy-start | bytes 786436
  0.0 39.5 %copy-start.3 = (s32[16,2048]{1,0:T(8,128)S(1)}, s32[16,2048]{1,0:T(8,128)}, u32[]{:S(2)}) copy-start(s32[16,2048]{1,0:T(8,128)} %mask_ref.1) | copy-start | bytes 393220
  0.1 0.9 %copy-start.4 = (f32[128,128]{1,0:T(8,128)S(1)}, f32[128,128]{1,0:T(8,128)}, u32[]{:S(2)}) copy-start(f32[128,128]{1,0:T(8,128)} %value_ref.1) | copy-start | bytes 196612
  1.0 0.8 %copy-start.5 = (f32[128,128]{1,0:T(8,128)S(1)}, f32[128,128]{1,0:T(8,128)}, u32[]{:S(2)}) copy-start(f32[128,128]{1,0:T(8,128)} %weight_ref.1) | copy-start | bytes 196612
  1.8 0.8 %copy-start.6 = (s32[128,128]{1,0:T(8,128)S(1)}, s32[128,128]{1,0:T(8,128)}, u32[]{:S(2)}) copy-start(s32[128,128]{1,0:T(8,128)} %cols_ref.1) | copy-start | bytes 196612
  2.7 0.7 %copy-start.11 = (s32[128,1]{0,1:T(1,128)S(1)}, s32[128,1]{0,1:T(1,128)}, u32[]{:S(2)}) copy-start(s32[128,1]{0,1:T(1,128)} %param.14) | copy-start | bytes 1540
  3.3 0.7 %copy-start.12 = (s32[128]{0:T(128)S(1)}, s32[128]{0:T(128)}, u32[]{:S(2)}) copy-start(s32[128]{0:T(128)} %row_ref.1) | copy-start | bytes 1540
  4.0 0.7 %copy-start.13 = (s32[128]{0:T(128)S(1)}, s32[128]{0:T(128)}, u32[]{:S(2)}) copy-start(s32[128]{0:T(128)} %sensor_ref.1) | copy-start | bytes 1540
  7.1 21.7 %all-to-all-start = ((f32[4,200,128]{2,1,0:T(8,128)}), f32[4,200,128]{2,1,0:T(8,128)S(1)}, u32[]{:S(2)}, u32[]{:S(2)}) async-start(f32[4,200,128]{2,1,0:T(8,128)} %shard_map.111), calls=%async_computation | async-start | bytes 819200 | tf_op jit(solution)/shard_map/all_to_all | solution.py:291
  13.4 0.9 %copy-start = (f32[2,16,2048]{2,1,0:T(8,128)S(1)}, f32[2,16,2048]{2,1,0:T(8,128)}, u32[]{:S(2)}) copy-start(f32[2,16,2048]{2,1,0:T(8,128)} %control_ref.3) | copy-start | bytes 786436
  14.3 0.7 %copy-start.7 = (f32[8,8]{1,0:T(8,128)S(1)}, f32[8,8]{1,0:T(8,128)}, u32[]{:S(2)}) copy-start(f32[8,8]{1,0:T(8,128)} %factor_ref.3) | copy-start | bytes 772
  15.0 0.7 %copy-start.9 = (f32[2,8]{1,0:T(2,128)S(1)}, f32[2,8]{1,0:T(2,128)}, u32[]{:S(2)}) copy-start(f32[2,8]{1,0:T(2,128)} %sens_ref.3) | copy-start | bytes 196
  16.4 1.4 %collective-permute-start = (f32[16,2048]{1,0:T(8,128)S(1)}, f32[16,2048]{1,0:T(8,128)S(1)}, u32[]{:S(2)}, u32[]{:S(2)}) collective-permute-start(f32[16,2048]{1,0:T(8,128)S(1)} %get-tuple-element.17), channel_id=1, source_target_pairs={{0,1},{1,0},{2,3},{3,2},{4,5},{5,4},{6,7},{7,6},{8,9},{9,8},{10,11... | collective-permute-start | bytes 393224 | tf_op jit(solution)/shard_map/ppermute | solution.py:257
  17.8 5.6 %collective-permute-start.1 = (f32[16,2048]{1,0:T(8,128)S(1)}, f32[16,2048]{1,0:T(8,128)S(1)}, u32[]{:S(2)}, u32[]{:S(2)}) collective-permute-start(f32[16,2048]{1,0:T(8,128)S(1)} %add.3.first_ref), channel_id=1, source_target_pairs={{0,2},{1,3},{2,0},{3,1},{4,6},{5,7},{6,4},{7,5},{8,10},{9,11},{10,... | collective-permute-start | bytes 393224 | tf_op jit(solution)/shard_map/ppermute | solution.py:257
  23.5 11.8 %collective-permute-start.2 = (f32[3,10,2048]{2,1,0:T(8,128)S(1)}, f32[3,10,2048]{2,1,0:T(8,128)S(1)}, u32[]{:S(2)}, u32[]{:S(2)}) collective-permute-start(f32[3,10,2048]{2,1,0:T(8,128)S(1)} %get-tuple-element.19), channel_id=1, source_target_pairs={{0,4},{4,8},{8,12},{1,5},{5,9},{9,13},{2,6},{6,10},{10,14},{3,7},{... | collective-permute-start | bytes 737288 | tf_op jit(solution)/shard_map/ppermute | solution.py:262
  27.5 12.0 %collective-permute-start.3 = (f32[3,10,2048]{2,1,0:T(8,128)S(1)}, f32[3,10,2048]{2,1,0:T(8,128)S(1)}, u32[]{:S(2)}, u32[]{:S(2)}) collective-permute-start(f32[3,10,2048]{2,1,0:T(8,128)S(1)} %get-tuple-element.20), channel_id=1, source_target_pairs={{4,0},{8,4},{12,8},{5,1},{9,5},{13,9},{6,2},{10,6},{14,10},{7,3},{... | collective-permute-start | bytes 737288 | tf_op jit(solution)/shard_map/ppermute | solution.py:263
  39.5 20.7 %copy-start.1 = (f32[2,16,2048]{2,1,0:T(8,128)S(1)}, f32[2,16,2048]{2,1,0:T(8,128)}, u32[]{:S(2)}) copy-start(f32[2,16,2048]{2,1,0:T(8,128)} %control_ref.3) | copy-start | bytes 786436
  39.5 20.7 %copy-start.8 = (f32[8,8]{1,0:T(8,128)S(1)}, f32[8,8]{1,0:T(8,128)}, u32[]{:S(2)}) copy-start(f32[8,8]{1,0:T(8,128)} %factor_ref.3) | copy-start | bytes 772
  39.5 20.7 %copy-start.10 = (f32[2,8]{1,0:T(2,128)S(1)}, f32[2,8]{1,0:T(2,128)}, u32[]{:S(2)}) copy-start(f32[2,8]{1,0:T(2,128)} %sens_ref.3) | copy-start | bytes 196
  44.3 5.9 %collective-permute-start.4 = (f32[10,2048]{1,0:T(8,128)S(1)}, f32[10,2048]{1,0:T(8,128)S(1)}, u32[]{:S(2)}, u32[]{:S(2)}) collective-permute-start(f32[10,2048]{1,0:T(8,128)S(1)} %get-tuple-element.24), channel_id=1, source_target_pairs={{0,4},{4,8},{8,12},{1,5},{5,9},{9,13},{2,6},{6,10},{10,14},{3,7},{... | collective-permute-start | bytes 245768 | tf_op jit(solution)/shard_map/ppermute | solution.py:262
  47.6 6.9 %collective-permute-start.5 = (f32[10,2048]{1,0:T(8,128)S(1)}, f32[10,2048]{1,0:T(8,128)S(1)}, u32[]{:S(2)}, u32[]{:S(2)}) collective-permute-start(f32[10,2048]{1,0:T(8,128)S(1)} %get-tuple-element.25), channel_id=1, source_target_pairs={{4,0},{8,4},{12,8},{5,1},{9,5},{13,9},{6,2},{10,6},{14,10},{7,3},{... | collective-permute-start | bytes 245768 | tf_op jit(solution)/shard_map/ppermute | solution.py:263
  58.7 1.4 %collective-permute-start.6 = (f32[16,2048]{1,0:T(8,128)S(1)}, f32[16,2048]{1,0:T(8,128)S(1)}, u32[]{:S(2)}, u32[]{:S(2)}) collective-permute-start(f32[16,2048]{1,0:T(8,128)S(1)} %shard_map.114.own_ref), channel_id=1, source_target_pairs={{0,1},{1,0},{2,3},{3,2},{4,5},{5,4},{6,7},{7,6},{8,9},{9,8},{10,11... | collective-permute-start | bytes 393224 | tf_op jit(solution)/shard_map/ppermute | solution.py:257

commit v2 on v1

v2 whole, which is shorter than its diff:
```python
import functools

import jax
import jax.numpy as jnp
from jax import lax
from jax.experimental import pallas as pl
from jax.experimental.pallas import tpu as pltpu
from jax.sharding import PartitionSpec as P

PASSES = 10
LANES = 128
GROUP = 8
VMEM = pl.BlockSpec(memory_space=pltpu.VMEM)
SMEM = pl.BlockSpec(memory_space=pltpu.SMEM)
HBM = pl.BlockSpec(memory_space=pltpu.HBM)
F32 = jnp.float32


def call(body, outs, ins, scratch=(), limit=16, cost=None):
    return pl.pallas_call(
        body,
        out_shape=outs,
        in_specs=ins,
        out_specs=[VMEM] * len(outs),
        scratch_shapes=list(scratch),
        compiler_params=pltpu.CompilerParams(vmem_limit_bytes=limit << 20),
        cost_estimate=cost,
    )


def cost(cycles):
    return pl.CostEstimate(flops=cycles * 4096, bytes_accessed=cycles * 1024, transcendentals=0)


def response(sens_ref, factor_ref, sensor, variable):
    total = sens_ref[sensor, 0] * factor_ref[0, variable]
    for u in range(1, factor_ref.shape[0]):
        total = total + sens_ref[sensor, u] * factor_ref[u, variable]
    return total


def first_kernel(slots, margin, pos_ref, sens_hbm, factor_hbm, control_hbm, kappa_hbm, tile_hbm, row_hbm,
                 sensor_hbm, value_hbm, weight_hbm, cols_hbm, *refs):
    outs, refs = refs[:4], refs[4:]
    own_ref, other_ref, even_ref, odd_ref = outs
    tiles = len(refs) - 13
    chunk_refs, refs = refs[:tiles], refs[tiles:]
    (sens_ref, factor_ref, control_ref, kappa_ref, tile_ref, row_ref, sensor_ref, value_ref, weight_ref,
     cols_ref, send_ref, count_ref, sems) = refs
    pairs = (
        (sens_hbm, sens_ref), (factor_hbm, factor_ref), (control_hbm, control_ref),
        (kappa_hbm, kappa_ref), (tile_hbm, tile_ref), (row_hbm, row_ref), (sensor_hbm, sensor_ref),
        (value_hbm, value_ref), (weight_hbm, weight_ref), (cols_hbm, cols_ref),
    )
    copies = [pltpu.make_async_copy(src, dst, sems.at[i]) for i, (src, dst) in enumerate(pairs)]
    for copy in copies:
        copy.start()
    send_ref[...] = jnp.zeros(send_ref.shape, F32)
    for t in range(tiles):
        count_ref[t] = 0
    for copy in copies:
        copy.wait()

    pos, mine = pos_ref[0], pos_ref[1]
    core = pos % 2
    var_dev = control_ref.shape[0]
    for sensor, out_ref in ((1 - core, other_ref), (core, own_ref)):
        total = None
        for v in range(var_dev):
            term = response(sens_ref, factor_ref, sensor, pos * var_dev + v) * control_ref[v]
            total = term if total is None else total + term
        out_ref[...] = total
    for i in range(2):
        pack_edges(even_ref.at[i], odd_ref.at[i], kappa_ref[i], margin, mine % 2 == 0)

    panels = value_ref.shape[0]
    pad_tiles = -(-tiles // 8) * 8
    sub = lax.broadcasted_iota(jnp.int32, (pad_tiles, LANES), 0)
    lane = lax.broadcasted_iota(jnp.int32, (pad_tiles, LANES), 1)

    def place(p, meta):
        t = tile_ref[p]
        keep = sensor_ref[p] == core
        slot = count_ref[t]
        count_ref[t] = slot + keep.astype(jnp.int32)
        trash = 3 * slots + 7
        rows = (value_ref[pl.ds(p, 1), :], weight_ref[pl.ds(p, 1), :], cols_ref[pl.ds(p, 1), :].astype(F32))
        for part, row in enumerate(rows):
            send_ref[t, pl.ds(jnp.where(keep, part * slots + slot, trash), 1), :] = row
        where = jnp.where(keep, slot, LANES)
        return jnp.where((sub == t) & (lane == where), row_ref[p].astype(F32), meta)

    meta = lax.fori_loop(0, panels, place, jnp.zeros((pad_tiles, LANES), F32), unroll=4)
    for t in range(tiles):
        meta = jnp.where((sub == t) & (lane == slots), count_ref[t].astype(F32), meta)
    for t in range(tiles):
        send_ref[t, pl.ds(3 * slots, 1), :] = meta[t : t + 1]
    for d in range(tiles):
        chunk_refs[d][...] = send_ref[mine ^ d]


def pieces(values):
    top = values.astype(jnp.bfloat16).astype(F32)
    return top, values - top


def scatter_kernel(slots, meta_ref, *refs):
    got_refs, (weight_out, value_out, acc_ref) = refs[:-3], refs[-3:]
    rows, width_cols = weight_out.shape
    blocks = width_cols // LANES
    acc_ref[...] = jnp.zeros(acc_ref.shape, F32)
    block_ids = lax.broadcasted_iota(jnp.int32, (blocks, LANES), 0)
    lane_ids = lax.broadcasted_iota(jnp.int32, (LANES, LANES), 0)
    sub = lax.broadcasted_iota(jnp.int32, (GROUP, LANES), 0)

    def source(s, got_ref):
        count = meta_ref[s, slots]

        def group(g, carry):
            base = pl.multiple_of(g * GROUP, GROUP)
            value = got_ref[pl.ds(base, GROUP), :]
            weight = got_ref[pl.ds(slots + base, GROUP), :]
            cell = got_ref[pl.ds(2 * slots + base, GROUP), :].astype(jnp.int32)
            weight = jnp.where(sub + base < count, weight, 0.0)
            parts = pieces(weight) + pieces(weight * value)
            low = cell % LANES
            high = cell // LANES
            for k in range(GROUP):
                in_block = block_ids == high[k : k + 1]
                left = jnp.concatenate(
                    [jnp.where(in_block, parts[i][k : k + 1], 0.0) for i in (0, 2, 1, 3)], axis=0
                ).astype(jnp.bfloat16)
                right = jnp.where(lane_ids == low[k : k + 1], 1.0, 0.0).astype(jnp.bfloat16)
                both = lax.dot_general(
                    left, right, (((1,), (1,)), ((), ())), preferred_element_type=F32
                )
                row = meta_ref[s, base + k]
                at = pl.ds(pl.multiple_of(row * 2 * blocks, 2 * blocks), 2 * blocks)
                acc_ref[at, :] += both[: 2 * blocks] + both[2 * blocks :]
            return carry

        lax.fori_loop(0, (count + GROUP - 1) // GROUP, group, 0)

    for s, got_ref in enumerate(got_refs):
        source(s, got_ref)
    for b in range(blocks):
        at = slice(b * LANES, (b + 1) * LANES)
        weight_out[:, at] = acc_ref[pl.ds(b, rows, stride=2 * blocks), :]
        value_out[:, at] = acc_ref[pl.ds(blocks + b, rows, stride=2 * blocks), :]


def pack_edges(even_ref, odd_ref, rows_value, margin, even):
    rows, width = rows_value.shape
    for b in range(width // LANES):
        at = slice(b * LANES, (b + 1) * LANES)
        head, tail = rows_value[:margin, at], rows_value[rows - margin :, at]
        even_ref[b * margin : (b + 1) * margin] = jnp.where(even, tail, head)
        odd_ref[b * margin : (b + 1) * margin] = jnp.where(even, head, tail)


def edges_kernel(margin, pos_ref, first_ref, second_ref, total_ref, even_ref, odd_ref):
    total = first_ref[...] + second_ref[...]
    total_ref[...] = total
    pack_edges(even_ref, odd_ref, total, margin, pos_ref[1] % 2 == 0)


def ring_rows(rows, margin):
    return -(-(rows + 2 * margin) // 8) * 8


def lay_ring(ref, own, from_even, from_odd, margin, even):
    rows, total = own.shape[0], ref.shape[0]
    ref[rows:total] = jnp.zeros((total - rows, ref.shape[1]), F32)
    ref[:rows] = own
    for b in range(ref.shape[1] // LANES):
        at = slice(b * LANES, (b + 1) * LANES)
        one, two = (m[b * margin : (b + 1) * margin] for m in (from_even, from_odd))
        ref[rows : rows + margin, at] = jnp.where(even, one, two)
        ref[total - margin :, at] = jnp.where(even, two, one)


def block(ref, j):
    return ref[:, j * LANES : (j + 1) * LANES]


def sideways(blocks):
    shape = blocks[0].shape
    lane = lax.broadcasted_iota(jnp.int32, shape, 1)
    zero = jnp.zeros(shape, F32)
    ahead = [pltpu.roll(x, 1, 1) for x in blocks]
    back = [pltpu.roll(x, LANES - 1, 1) for x in blocks]
    for j, here in enumerate(blocks):
        before = ahead[j - 1] if j else zero
        after = back[j + 1] if j + 1 < len(blocks) else zero
        yield here, jnp.where(lane == 0, before, ahead[j]), jnp.where(lane == LANES - 1, after, back[j])


def face_weights(coef_ref, row_ref, col_ref, rows, margin, has_above, has_below):
    total, width = row_ref.shape
    blocks = width // LANES
    r = lax.broadcasted_iota(jnp.int32, (total, LANES), 0)
    inside = (
        (r < rows)
        | ((r < rows + margin) & has_below)
        | ((r >= total - margin) & has_above)
    )
    scale = jnp.where(inside, 0.125, 0.0)
    unit = jnp.where(inside, 1.0, 0.0)
    columns = [block(col_ref, j) for j in range(blocks)]
    for j, (k_col, k_left, k_right) in enumerate(sideways(columns)):
        at = slice(j * LANES, (j + 1) * LANES)
        k_row = block(row_ref, j)
        up = scale * (k_row + pltpu.roll(k_row, 1, 0))
        down = scale * (k_row + pltpu.roll(k_row, total - 1, 0))
        left = scale * (k_col + k_left)
        right = scale * (k_col + k_right)
        coef_ref[0, :, at] = unit - up - down - left - right
        coef_ref[1, :, at] = up
        coef_ref[2, :, at] = down
        coef_ref[3, :, at] = left
        coef_ref[4, :, at] = right


def one_pass(source_ref, target_ref, coef_ref, spans, keep):
    width = source_ref.shape[1]

    def read(ref, *lead, at):
        got = [ref[(*lead, span, at)] for span in spans]
        return jnp.concatenate(got, axis=0) if len(got) > 1 else got[0]

    sections = [slice(j * LANES, (j + 1) * LANES) for j in range(width // LANES)]
    fields = [read(source_ref, at=at) for at in sections]
    total = fields[0].shape[0]
    for at, (here, left, right) in zip(sections, sideways(fields)):
        new = (
            read(coef_ref, 0, at=at) * here
            + read(coef_ref, 1, at=at) * pltpu.roll(here, 1, 0)
            + read(coef_ref, 2, at=at) * pltpu.roll(here, total - 1, 0)
            + read(coef_ref, 3, at=at) * left
            + read(coef_ref, 4, at=at) * right
        )
        start = 0
        for span in spans[:keep]:
            size = span.stop - span.start
            target_ref[span, at] = new[start : start + size]
            start += size


def diffuse(one_ref, two_ref, coef_ref, rows, margin):
    total = one_ref.shape[0]
    wide = [slice(0, total)]
    inner = margin // 8 * 8
    narrow = [slice(0, rows), slice(rows, rows + inner), slice(total - inner, total)]
    first = (margin - inner + 1) // 2

    def twice(spans, index, carry):
        one_pass(one_ref, two_ref, coef_ref, spans, len(spans))
        one_pass(two_ref, one_ref, coef_ref, spans, len(spans))
        return carry

    for i in range(first):
        twice(wide, i, 0)
    lax.fori_loop(0, PASSES // 2 - first - 1, functools.partial(twice, narrow), 0)
    one_pass(one_ref, two_ref, coef_ref, narrow, 3)
    one_pass(two_ref, one_ref, coef_ref, narrow, 1)


def analyse_kernel(tiles, margin, pos_ref, own_ref, even_ref, odd_ref, kappa_ref, kappa_even_ref,
                   kappa_odd_ref, mask_ref, weight_ref, value_ref, coef_ref, adjoint_ref, even_out,
                   odd_out, one_ref, two_ref):
    rows = own_ref.shape[0]
    tile = pos_ref[1]
    even = tile % 2 == 0
    lay_ring(one_ref, kappa_ref[0], kappa_even_ref.at[0], kappa_odd_ref.at[0], margin, even)
    lay_ring(two_ref, kappa_ref[1], kappa_even_ref.at[1], kappa_odd_ref.at[1], margin, even)
    face_weights(coef_ref, one_ref, two_ref, rows, margin, tile > 0, tile + 1 < tiles)
    lay_ring(one_ref, own_ref[...], even_ref, odd_ref, margin, even)
    diffuse(one_ref, two_ref, coef_ref, rows, margin)
    adjoint = mask_ref[...].astype(F32) * (weight_ref[...] * one_ref[:rows] - value_ref[...])
    adjoint_ref[...] = adjoint
    pack_edges(even_out, odd_out, adjoint, margin, even)


def spread_kernel(margin, pos_ref, own_ref, even_ref, odd_ref, coef_ref, out_ref, one_ref, two_ref):
    rows = own_ref.shape[0]
    lay_ring(one_ref, own_ref[...], even_ref, odd_ref, margin, pos_ref[1] % 2 == 0)
    diffuse(one_ref, two_ref, coef_ref, rows, margin)
    out_ref[...] = one_ref[:rows]


def result_kernel(pos_ref, sens_ref, factor_ref, control_ref, own_ref, other_ref, out_ref):
    var_dev = control_ref.shape[0]
    pos = pos_ref[0]
    core = pos % 2
    for v in range(var_dev):
        mine = response(sens_ref, factor_ref, core, pos * var_dev + v)
        theirs = response(sens_ref, factor_ref, 1 - core, pos * var_dev + v)
        out_ref[v] = control_ref[v] + mine * own_ref[...] + theirs * other_ref[...]


def swap(values, axis, bit):
    count = lax.axis_size(axis)
    return lax.ppermute(values, axis, [(i, i ^ bit) for i in range(count)])


def swap_edges(even, odd):
    count = lax.axis_size("tile")
    later = [(i, i + 1) for i in range(1, count - 1, 2)]
    later += [(b, a) for a, b in later]
    return swap(even, "tile", 1), lax.ppermute(odd, "tile", later)


def local(control, diffusivity, land_mask, panel_tile, panel_row, panel_cols, obs_values,
          obs_weights, panel_sensor, sensitivity, cross_factor):
    rows, width = control.shape[1:]
    tiles, members = lax.axis_size("tile"), lax.axis_size("var")
    panels, panel_width = panel_cols.shape
    slots = 2 * panels // tiles
    blocks = width // LANES
    margin = PASSES
    total = ring_rows(rows, margin)
    field = jax.ShapeDtypeStruct((rows, width), F32)
    edge = jax.ShapeDtypeStruct((margin * blocks, LANES), F32)
    edge2 = jax.ShapeDtypeStruct((2, margin * blocks, LANES), F32)
    chunk = jax.ShapeDtypeStruct((3 * slots + 8, panel_width), F32)
    pos = jnp.stack([lax.axis_index("var"), lax.axis_index("tile")]).astype(jnp.int32)

    own, other, kappa_even, kappa_odd, *chunks = call(
        functools.partial(first_kernel, slots, margin),
        [field, field, edge2, edge2] + [chunk] * tiles,
        [SMEM] + [HBM] * 10,
        [
            pltpu.SMEM(sensitivity.shape, F32),
            pltpu.SMEM(cross_factor.shape, F32),
            pltpu.VMEM(control.shape, F32),
            pltpu.VMEM(diffusivity.shape, F32),
            pltpu.SMEM((panels,), jnp.int32),
            pltpu.SMEM((panels,), jnp.int32),
            pltpu.SMEM((panels,), jnp.int32),
            pltpu.VMEM(obs_values.shape, F32),
            pltpu.VMEM(obs_weights.shape, F32),
            pltpu.VMEM(panel_cols.shape, jnp.int32),
            pltpu.VMEM((tiles, *chunk.shape), F32),
            pltpu.SMEM((tiles,), jnp.int32),
            pltpu.SemaphoreType.DMA((10,)),
        ],
        cost=cost(4000),
    )(pos, sensitivity, cross_factor, control, diffusivity, panel_tile.reshape(-1), panel_row,
      panel_sensor, obs_values, obs_weights, panel_cols)

    part = own + swap(other, "var", 1)
    got = [chunks[0]] + [swap(chunks[d], "tile", d) for d in range(1, tiles)]
    kappa_even, kappa_odd = swap_edges(kappa_even, kappa_odd)
    bit = 2
    while 2 * bit < members:
        part = part + swap(part, "var", bit)
        bit *= 2
    smooth_in, even, odd = call(
        functools.partial(edges_kernel, margin),
        [field, edge, edge],
        [SMEM] + [VMEM] * 2,
        cost=cost(500),
    )(pos, part, swap(part, "var", bit))
    even, odd = swap_edges(even, odd)

    meta = jnp.stack([g[3 * slots] for g in got]).astype(jnp.int32)
    weight_sum, value_sum = call(
        functools.partial(scatter_kernel, slots),
        [field, field],
        [SMEM] + [VMEM] * tiles,
        [pltpu.VMEM((rows * 2 * blocks, LANES), F32)],
        cost=cost(10000),
    )(meta, *got)

    ring = pltpu.VMEM((total, width), F32)
    coef, adjoint, even, odd = call(
        functools.partial(analyse_kernel, tiles, margin),
        [jax.ShapeDtypeStruct((5, total, width), F32), field, edge, edge],
        [SMEM] + [VMEM] * 9,
        [ring, ring],
        cost=cost(5000),
    )(pos, smooth_in, even, odd, diffusivity, kappa_even, kappa_odd, land_mask, weight_sum, value_sum)
    even, odd = swap_edges(even, odd)
    (mine,) = call(
        functools.partial(spread_kernel, margin),
        [field],
        [SMEM] + [VMEM] * 4,
        [ring, ring],
        cost=cost(4000),
    )(pos, adjoint, even, odd, coef)
    (out,) = call(
        result_kernel,
        [jax.ShapeDtypeStruct(control.shape, F32)],
        [SMEM] * 3 + [VMEM] * 3,
        cost=cost(1000),
    )(pos, sensitivity, cross_factor, control, mine, swap(mine, "var", 1))
    return out


def solution(mesh):
    return jax.shard_map(
        local,
        mesh=mesh,
        in_specs=(
            P("var", ("grp", "tile"), None),
            P(None, ("grp", "tile"), None),
            P(("grp", "tile"), None),
            P(("grp", "tile"), None),
            P(("grp", "tile")),
            P(("grp", "tile"), None),
            P(("grp", "tile"), None),
            P(("grp", "tile"), None),
            P(("grp", "tile")),
            P(),
            P(),
        ),
        out_specs=P("var", ("grp", "tile"), None),
        check_vma=False,
    )
```

time: 62 us -> 51.3 us (0.83)
  the two profiles are of different devices: /device:TPU:0 before, /device:TPU:13 now
where the time goes in v2:
time: 51.3 us; the launch traced here: 50.9 us
  starting transfers between devices  21.3 us (42%)
  Pallas kernels  13.7 us (27%)
  waiting for transfers between devices  7.83 us (15%)
  local copies, waits for them, and re-layouts  7.78 us (15%)
    ppermute x3, starting transfers between devices, swap_edges(): return (swap(even, 'tile', 1), lax.ppermute(odd, 'tile', later))  12 us
    ppermute x9, starting transfers between devices, swap(): return lax.ppermute(values, axis, [(i, i ^ bit) for i in range(count)])  9.29 us
    unnamed x30, local copies, waits for them, and re-layouts  7.77 us
    ppermute x9, waiting for transfers between devices, swap(): return lax.ppermute(values, axis, [(i, i ^ bit) for i in range(count)])  6.02 us
    pallas_call x1, Pallas kernels, local(): call(functools.partial(analyse_kernel, tiles, margin), [jax.ShapeDtypeStr...  3.22 us
    pallas_call x1, Pallas kernels, local(): call(functools.partial(scatter_kernel, slots), [field, field], [SMEM] + [...  3.1 us
    pallas_call x1, Pallas kernels, local(): call(functools.partial(spread_kernel, margin), [field], [SMEM] + [VMEM] *...  2.84 us
    pallas_call x1, Pallas kernels, local(): call(functools.partial(first_kernel, slots, margin), [field, field, edge2...  2.53 us
  transfers between devices with their start and end apart: 12, of which 5 were waited for; matrix products, arithmetic and copies ran while one was open for 0% of the time, Pallas kernels for 7%

profile of v2, /device:TPU:13, one launch (start us, length us, event | category | flops | bytes accessed | tf_op | source)
XLA Modules:
  0.0 50.9 jit_solution(17318506339403552709)
XLA Ops:
  0.0 0.1 pad_add_fusion.pos_ref
  0.1 0.9 %copy-done = f32[2,16,2048]{2,1,0:T(8,128)S(1)} copy-done((f32[2,16,2048]{2,1,0:T(8,128)S(1)}, f32[2,16,2048]{2,1,0:T(8,128)}, u32[]{:S(2)}) %copy-start) | copy-done | bytes 262168
  1.0 0.9 %copy-done.2 = f32[2,16,2048]{2,1,0:T(8,128)S(1)} copy-done((f32[2,16,2048]{2,1,0:T(8,128)S(1)}, f32[2,16,2048]{2,1,0:T(8,128)}, u32[]{:S(2)}) %copy-start.2) | copy-done | bytes 262168
  2.0 0.8 %copy-done.5 = f32[128,128]{1,0:T(8,128)S(1)} copy-done((f32[128,128]{1,0:T(8,128)S(1)}, f32[128,128]{1,0:T(8,128)}, u32[]{:S(2)}) %copy-start.5) | copy-done | bytes 65560
  2.8 0.8 %copy-done.6 = f32[128,128]{1,0:T(8,128)S(1)} copy-done((f32[128,128]{1,0:T(8,128)S(1)}, f32[128,128]{1,0:T(8,128)}, u32[]{:S(2)}) %copy-start.6) | copy-done | bytes 65560
  3.7 0.8 %copy-done.7 = s32[128,128]{1,0:T(8,128)S(1)} copy-done((s32[128,128]{1,0:T(8,128)S(1)}, s32[128,128]{1,0:T(8,128)}, u32[]{:S(2)}) %copy-start.7) | copy-done | bytes 65560
  4.5 0.7 %copy-done.8 = f32[8,8]{1,0:T(8,128)S(1)} copy-done((f32[8,8]{1,0:T(8,128)S(1)}, f32[8,8]{1,0:T(8,128)}, u32[]{:S(2)}) %copy-start.8) | copy-done | bytes 280
  5.2 0.7 %copy-done.10 = f32[2,8]{1,0:T(2,128)S(1)} copy-done((f32[2,8]{1,0:T(2,128)S(1)}, f32[2,8]{1,0:T(2,128)}, u32[]{:S(2)}) %copy-start.10) | copy-done | bytes 88
  5.9 0.7 %copy-done.12 = s32[128,1]{0,1:T(1,128)S(1)} copy-done((s32[128,1]{0,1:T(1,128)S(1)}, s32[128,1]{0,1:T(1,128)}, u32[]{:S(2)}) %copy-start.12) | copy-done | bytes 536
  6.5 0.7 %copy-done.13 = s32[128]{0:T(128)S(1)} copy-done((s32[128]{0:T(128)S(1)}, s32[128]{0:T(128)}, u32[]{:S(2)}) %copy-start.13) | copy-done | bytes 536
  7.2 0.7 %copy-done.14 = s32[128]{0:T(128)S(1)} copy-done((s32[128]{0:T(128)S(1)}, s32[128]{0:T(128)}, u32[]{:S(2)}) %copy-start.14) | copy-done | bytes 536
  7.8 2.5 %shard_map.109 = (f32[16,2048]{1,0:T(8,128)S(1)}, f32[16,2048]{1,0:T(8,128)S(1)}, f32[2,160,128]{2,1,0:T(8,128)S(1)}, f32[2,160,128]{2,1,0:T(8,128)S(1)}, f32[20...) custom-call(s32[2]{0:T(128)S(1)} %pad_add_fusion.pos_ref, ...), custom_call_target="tpu_custom_call" | custom-call | flops 16384000 | bytes 4096000 | tf_op jit(solution)/shard_map/pallas_call | solution.py:328
  10.4 0.7 %collective-permute-start = (f32[16,2048]{1,0:T(8,128)S(1)}, f32[16,2048]{1,0:T(8,128)S(1)}, u32[]{:S(2)}, u32[]{:S(2)}) collective-permute-start(f32[16,2048]{1,0:T(8,128)S(1)} %get-tuple-element.23), channel_id=1, source_target_pairs={{0,1},{1,0},{2,3},{3,2},{4,5},{5,4},{6,7},{7,6},{8,9},{9,8},{10,11... | collective-permute-start | bytes 393224 | tf_op jit(solution)/shard_map/ppermute | solution.py:303
  11.1 0.2 collective-permute-start.6
  11.3 0.8 %collective-permute-done = f32[16,2048]{1,0:T(8,128)S(1)} collective-permute-done((f32[16,2048]{1,0:T(8,128)S(1)}, f32[16,2048]{1,0:T(8,128)S(1)}, u32[]{:S(2)}, u32[]{:S(2)}) %collective-permute-start) | collective-permute-done | bytes 131104 | tf_op jit(solution)/shard_map/ppermute | solution.py:303
  12.1 1.3 %collective-permute-start.1 = (f32[16,2048]{1,0:T(8,128)S(1)}, f32[16,2048]{1,0:T(8,128)S(1)}, u32[]{:S(2)}, u32[]{:S(2)}) collective-permute-start(f32[16,2048]{1,0:T(8,128)S(1)} %add.3.first_ref), channel_id=1, source_target_pairs={{0,2},{1,3},{2,0},{3,1},{4,6},{5,7},{6,4},{7,5},{8,10},{9,11},{10,... | collective-permute-start | bytes 393224 | tf_op jit(solution)/shard_map/ppermute | solution.py:303
  13.4 2.3 %collective-permute-start.7 = (f32[200,128]{1,0:T(8,128)S(1)}, f32[200,128]{1,0:T(8,128)S(1)}, u32[]{:S(2)}, u32[]{:S(2)}) collective-permute-start(f32[200,128]{1,0:T(8,128)S(1)} %get-tuple-element.31), channel_id=1, source_target_pairs={{0,8},{4,12},{8,0},{12,4},{1,9},{5,13},{9,1},{13,5},{2,10},{6,14},... | collective-permute-start | bytes 307208 | tf_op jit(solution)/shard_map/ppermute | solution.py:303
  15.7 1.2 %collective-permute-start.4 = (f32[2,160,128]{2,1,0:T(8,128)S(1)}, f32[2,160,128]{2,1,0:T(8,128)S(1)}, u32[]{:S(2)}, u32[]{:S(2)}) collective-permute-start(f32[2,160,128]{2,1,0:T(8,128)S(1)} %get-tuple-element.27), channel_id=1, source_target_pairs={{0,4},{4,0},{8,12},{12,8},{1,5},{5,1},{9,13},{13,9},{2,6},{6,2},{1... | collective-permute-start | bytes 491528 | tf_op jit(solution)/shard_map/ppermute | solution.py:303
  16.9 3.5 %collective-permute-start.5 = (f32[2,160,128]{2,1,0:T(8,128)S(1)}, f32[2,160,128]{2,1,0:T(8,128)S(1)}, u32[]{:S(2)}, u32[]{:S(2)}) collective-permute-start(f32[2,160,128]{2,1,0:T(8,128)S(1)} %get-tuple-element.28), channel_id=1, source_target_pairs={{4,8},{8,4},{5,9},{9,5},{6,10},{10,6},{7,11},{11,7},{20,24},{24,20... | collective-permute-start | bytes 491528 | tf_op jit(solution)/shard_map/ppermute | solution.py:310
  20.5 1.9 %collective-permute-done.7.refs_2_ = f32[200,128]{1,0:T(8,128)S(1)} collective-permute-done((f32[200,128]{1,0:T(8,128)S(1)}, f32[200,128]{1,0:T(8,128)S(1)}, u32[]{:S(2)}, u32[]{:S(2)}) %collective-permute-start.7) | collective-permute-done | bytes 102432 | tf_op jit(solution)/shard_map/ppermute | solution.py:303
  22.4 2.3 %collective-permute-done.8.refs_3_ = f32[200,128]{1,0:T(8,128)S(1)} collective-permute-done((f32[200,128]{1,0:T(8,128)S(1)}, f32[200,128]{1,0:T(8,128)S(1)}, u32[]{:S(2)}, u32[]{:S(2)}) %collective-permute-start.8) | collective-permute-done | bytes 102432 | tf_op jit(solution)/shard_map/ppermute | solution.py:303
  24.7 0.6 %shard_map.110 = (f32[16,2048]{1,0:T(8,128)S(1)}, f32[160,128]{1,0:T(8,128)S(1)}, f32[160,128]{1,0:T(8,128)S(1)}) custom-call(s32[2]{0:T(128)S(1)} %pad_add_fusion.pos_ref, f32[16,2048]{1,0:T(8,128)S(1)} %add.3.first_ref, f32[16,2048]{1,0:T(8,128)S(1)} %collective-permute-done.1.second_ref), custom_call_target="tpu_custom_call" | custom-call | flops 2048000 | bytes 512000 | tf_op jit(solution)/shard_map/pallas_call | solution.py:358
  25.3 0.1 collective-permute-start.2
  25.4 4.1 %collective-permute-start.3 = (f32[160,128]{1,0:T(8,128)S(1)}, f32[160,128]{1,0:T(8,128)S(1)}, u32[]{:S(2)}, u32[]{:S(2)}) collective-permute-start(f32[160,128]{1,0:T(8,128)S(1)} %get-tuple-element.26), channel_id=1, source_target_pairs={{4,8},{8,4},{5,9},{9,5},{6,10},{10,6},{7,11},{11,7},{20,24},{24,20... | collective-permute-start | bytes 245768 | tf_op jit(solution)/shard_map/ppermute | solution.py:310
  29.5 3.1 %shard_map.111 = (f32[16,2048]{1,0:T(8,128)S(1)}, f32[16,2048]{1,0:T(8,128)S(1)}) custom-call(s32[4,128]{1,0:T(4,128)S(1)} %maximum_convert_fusion.meta_ref, f32[200,128]{1,0:T(8,128)S(1)} %get-tuple-element.29.refs_0_, f32[200,128]{1,0:T(8,128)S(1)} %collective-permute-done.6.refs_1_, f32[200,128]{1,0:T(8,128)S(1)} %collective-permute-done.7.refs_2_, ...), custom_call_target="tpu_custom_call" | custom-call | flops 40960000 | bytes 10240000 | tf_op jit(solution)/shard_map/pallas_call | solution.py:367
  32.7 3.2 %shard_map.112 = (f32[5,40,2048]{2,1,0:T(8,128)S(1)}, f32[16,2048]{1,0:T(8,128)S(1)}, f32[160,128]{1,0:T(8,128)S(1)}, f32[160,128]{1,0:T(8,128)S(1)}) custom-call(s32[2]{0:T(128)S(1)} %pad_add_fusion.pos_ref, f32[16,2048]{1,0:T(8,128)S(1)} %get-tuple-element.24.own_ref, f32[160,128]{1,0:T(8,128)S(1)} %collective-permute-done.2.even_ref, ...), custom_call_target="tpu_custom_call" | custom-call | flops 20480000 | bytes 5120000 | tf_op jit(solution)/shard_map/pallas_call | solution.py:376
  36.0 4.4 %collective-permute-start.10 = (f32[160,128]{1,0:T(8,128)S(1)}, f32[160,128]{1,0:T(8,128)S(1)}, u32[]{:S(2)}, u32[]{:S(2)}) collective-permute-start(f32[160,128]{1,0:T(8,128)S(1)} %get-tuple-element.37), channel_id=1, source_target_pairs={{4,8},{8,4},{5,9},{9,5},{6,10},{10,6},{7,11},{11,7},{20,24},{24,20... | collective-permute-start | bytes 245768 | tf_op jit(solution)/shard_map/ppermute | solution.py:310
  40.5 1.8 %collective-permute-done.10.odd_ref = f32[160,128]{1,0:T(8,128)S(1)} collective-permute-done((f32[160,128]{1,0:T(8,128)S(1)}, f32[160,128]{1,0:T(8,128)S(1)}, u32[]{:S(2)}, u32[]{:S(2)}) %collective-permute-start.10) | collective-permute-done | bytes 81952 | tf_op jit(solution)/shard_map/ppermute | solution.py:310
  42.3 2.8 %shard_map.113.own_ref = f32[16,2048]{1,0:T(8,128)S(1)} custom-call(s32[2]{0:T(128)S(1)} %pad_add_fusion.pos_ref, f32[16,2048]{1,0:T(8,128)S(1)} %get-tuple-element.35.own_ref, f32[160,128]{1,0:T(8,128)S(1)} %collective-permute-done.9.even_ref, f32[160,128]{1,0:T(8,128)S(1)} %collective-permute-done.10.odd_ref, f32[5,40,2048]{2,1,0:T(8,128)S(1)} %get-tuple-element.38.coef_ref), custom_call_target="tpu_custom_call" | custom-call | flops 16384000 | bytes 4096000 | tf_op jit(solution)/shard_map/pallas_call | solution.py:384
  45.1 3.4 %collective-permute-start.11 = (f32[16,2048]{1,0:T(8,128)S(1)}, f32[16,2048]{1,0:T(8,128)S(1)}, u32[]{:S(2)}, u32[]{:S(2)}) collective-permute-start(f32[16,2048]{1,0:T(8,128)S(1)} %shard_map.113.own_ref), channel_id=1, source_target_pairs={{0,1},{1,0},{2,3},{3,2},{4,5},{5,4},{6,7},{7,6},{8,9},{9,8},{10,11... | collective-permute-start | bytes 393224 | tf_op jit(solution)/shard_map/ppermute | solution.py:303
  48.5 1.0 %collective-permute-done.11.other_ref = f32[16,2048]{1,0:T(8,128)S(1)} collective-permute-done((f32[16,2048]{1,0:T(8,128)S(1)}, f32[16,2048]{1,0:T(8,128)S(1)}, u32[]{:S(2)}, u32[]{:S(2)}) %collective-permute-start.11) | collective-permute-done | bytes 131104 | tf_op jit(solution)/shard_map/ppermute | solution.py:303
  49.5 1.4 %shard_map.114 = f32[2,16,2048]{2,1,0:T(8,128)} custom-call(s32[2]{0:T(128)S(1)} %pad_add_fusion.pos_ref, f32[2,8]{1,0:T(2,128)S(1)} %copy-done.11, f32[8,8]{1,0:T(8,128)S(1)} %copy-done.9, f32[2,16,2048]{2,1,0:T(8,128)S(1)} %copy-done.1, f32[16,2048]{1,0:T(8,128)S(1)} %shard_map.113.own_ref, f32[16,2048]{1,0:T(8,128)S(1)} %collective-permute-done.11.other_ref), custom_call_target="tpu_custom_call" | custom-call | flops 4096000 | bytes 1024000 | tf_op jit(solution)/shard_map/pallas_call | solution.py:391
  (35 shorter events, 0.2 us)
Async XLA Ops:
  0.1 0.9 %copy-start = (f32[2,16,2048]{2,1,0:T(8,128)S(1)}, f32[2,16,2048]{2,1,0:T(8,128)}, u32[]{:S(2)}) copy-start(f32[2,16,2048]{2,1,0:T(8,128)} %control_ref.1) | copy-start | bytes 786436
  1.0 0.9 %copy-start.2 = (f32[2,16,2048]{2,1,0:T(8,128)S(1)}, f32[2,16,2048]{2,1,0:T(8,128)}, u32[]{:S(2)}) copy-start(f32[2,16,2048]{2,1,0:T(8,128)} %kappa_ref.1) | copy-start | bytes 786436
  2.0 0.8 %copy-start.5 = (f32[128,128]{1,0:T(8,128)S(1)}, f32[128,128]{1,0:T(8,128)}, u32[]{:S(2)}) copy-start(f32[128,128]{1,0:T(8,128)} %value_hbm.1) | copy-start | bytes 196612
  2.8 0.8 %copy-start.6 = (f32[128,128]{1,0:T(8,128)S(1)}, f32[128,128]{1,0:T(8,128)}, u32[]{:S(2)}) copy-start(f32[128,128]{1,0:T(8,128)} %weight_hbm.1) | copy-start | bytes 196612
  3.7 0.8 %copy-start.7 = (s32[128,128]{1,0:T(8,128)S(1)}, s32[128,128]{1,0:T(8,128)}, u32[]{:S(2)}) copy-start(s32[128,128]{1,0:T(8,128)} %cols_hbm.1) | copy-start | bytes 196612
  4.5 0.7 %copy-start.8 = (f32[8,8]{1,0:T(8,128)S(1)}, f32[8,8]{1,0:T(8,128)}, u32[]{:S(2)}) copy-start(f32[8,8]{1,0:T(8,128)} %factor_ref.1) | copy-start | bytes 772
  5.2 0.7 %copy-start.10 = (f32[2,8]{1,0:T(2,128)S(1)}, f32[2,8]{1,0:T(2,128)}, u32[]{:S(2)}) copy-start(f32[2,8]{1,0:T(2,128)} %sens_ref.1) | copy-start | bytes 196
  5.9 0.7 %copy-start.12 = (s32[128,1]{0,1:T(1,128)S(1)}, s32[128,1]{0,1:T(1,128)}, u32[]{:S(2)}) copy-start(s32[128,1]{0,1:T(1,128)} %param.14) | copy-start | bytes 1540
  6.5 0.7 %copy-start.13 = (s32[128]{0:T(128)S(1)}, s32[128]{0:T(128)}, u32[]{:S(2)}) copy-start(s32[128]{0:T(128)} %row_hbm.1) | copy-start | bytes 1540
  7.2 0.7 %copy-start.14 = (s32[128]{0:T(128)S(1)}, s32[128]{0:T(128)}, u32[]{:S(2)}) copy-start(s32[128]{0:T(128)} %sensor_hbm.1) | copy-start | bytes 1540
  7.8 24.8 %copy-start.3 = (f32[2,16,2048]{2,1,0:T(8,128)S(1)}, f32[2,16,2048]{2,1,0:T(8,128)}, u32[]{:S(2)}) copy-start(f32[2,16,2048]{2,1,0:T(8,128)} %kappa_ref.1) | copy-start | bytes 786436
  7.8 24.8 %copy-start.4 = (s32[16,2048]{1,0:T(8,128)S(1)}, s32[16,2048]{1,0:T(8,128)}, u32[]{:S(2)}) copy-start(s32[16,2048]{1,0:T(8,128)} %mask_ref.1) | copy-start | bytes 393220
  10.4 1.7 %collective-permute-start = (f32[16,2048]{1,0:T(8,128)S(1)}, f32[16,2048]{1,0:T(8,128)S(1)}, u32[]{:S(2)}, u32[]{:S(2)}) collective-permute-start(f32[16,2048]{1,0:T(8,128)S(1)} %get-tuple-element.23), channel_id=1, source_target_pairs={{0,1},{1,0},{2,3},{3,2},{4,5},{5,4},{6,7},{7,6},{8,9},{9,8},{10,11... | collective-permute-start | bytes 393224 | tf_op jit(solution)/shard_map/ppermute | solution.py:303
  11.1 5.8 %collective-permute-start.6 = (f32[200,128]{1,0:T(8,128)S(1)}, f32[200,128]{1,0:T(8,128)S(1)}, u32[]{:S(2)}, u32[]{:S(2)}) collective-permute-start(f32[200,128]{1,0:T(8,128)S(1)} %get-tuple-element.30), channel_id=1, source_target_pairs={{0,4},{4,0},{8,12},{12,8},{1,5},{5,1},{9,13},{13,9},{2,6},{6,2},{1... | collective-permute-start | bytes 307208 | tf_op jit(solution)/shard_map/ppermute | solution.py:303
  12.1 12.6 %collective-permute-start.1 = (f32[16,2048]{1,0:T(8,128)S(1)}, f32[16,2048]{1,0:T(8,128)S(1)}, u32[]{:S(2)}, u32[]{:S(2)}) collective-permute-start(f32[16,2048]{1,0:T(8,128)S(1)} %add.3.first_ref), channel_id=1, source_target_pairs={{0,2},{1,3},{2,0},{3,1},{4,6},{5,7},{6,4},{7,5},{8,10},{9,11},{10,... | collective-permute-start | bytes 393224 | tf_op jit(solution)/shard_map/ppermute | solution.py:303
  13.4 9.0 %collective-permute-start.7 = (f32[200,128]{1,0:T(8,128)S(1)}, f32[200,128]{1,0:T(8,128)S(1)}, u32[]{:S(2)}, u32[]{:S(2)}) collective-permute-start(f32[200,128]{1,0:T(8,128)S(1)} %get-tuple-element.31), channel_id=1, source_target_pairs={{0,8},{4,12},{8,0},{12,4},{1,9},{5,13},{9,1},{13,5},{2,10},{6,14},... | collective-permute-start | bytes 307208 | tf_op jit(solution)/shard_map/ppermute | solution.py:303
  15.7 9.0 %collective-permute-start.8 = (f32[200,128]{1,0:T(8,128)S(1)}, f32[200,128]{1,0:T(8,128)S(1)}, u32[]{:S(2)}, u32[]{:S(2)}) collective-permute-start(f32[200,128]{1,0:T(8,128)S(1)} %get-tuple-element.32), channel_id=1, source_target_pairs={{0,12},{4,8},{8,4},{12,0},{1,13},{5,9},{9,5},{13,1},{2,14},{6,10},... | collective-permute-start | bytes 307208 | tf_op jit(solution)/shard_map/ppermute | solution.py:303
  15.7 16.9 %collective-permute-start.4 = (f32[2,160,128]{2,1,0:T(8,128)S(1)}, f32[2,160,128]{2,1,0:T(8,128)S(1)}, u32[]{:S(2)}, u32[]{:S(2)}) collective-permute-start(f32[2,160,128]{2,1,0:T(8,128)S(1)} %get-tuple-element.27), channel_id=1, source_target_pairs={{0,4},{4,0},{8,12},{12,8},{1,5},{5,1},{9,13},{13,9},{2,6},{6,2},{1... | collective-permute-start | bytes 491528 | tf_op jit(solution)/shard_map/ppermute | solution.py:303
  16.9 15.7 %collective-permute-start.5 = (f32[2,160,128]{2,1,0:T(8,128)S(1)}, f32[2,160,128]{2,1,0:T(8,128)S(1)}, u32[]{:S(2)}, u32[]{:S(2)}) collective-permute-start(f32[2,160,128]{2,1,0:T(8,128)S(1)} %get-tuple-element.28), channel_id=1, source_target_pairs={{4,8},{8,4},{5,9},{9,5},{6,10},{10,6},{7,11},{11,7},{20,24},{24,20... | collective-permute-start | bytes 491528 | tf_op jit(solution)/shard_map/ppermute | solution.py:310
  25.3 7.3 %collective-permute-start.2 = (f32[160,128]{1,0:T(8,128)S(1)}, f32[160,128]{1,0:T(8,128)S(1)}, u32[]{:S(2)}, u32[]{:S(2)}) collective-permute-start(f32[160,128]{1,0:T(8,128)S(1)} %get-tuple-element.25), channel_id=1, source_target_pairs={{0,4},{4,0},{8,12},{12,8},{1,5},{5,1},{9,13},{13,9},{2,6},{6,2},{1... | collective-permute-start | bytes 245768 | tf_op jit(solution)/shard_map/ppermute | solution.py:303
  25.4 7.3 %collective-permute-start.3 = (f32[160,128]{1,0:T(8,128)S(1)}, f32[160,128]{1,0:T(8,128)S(1)}, u32[]{:S(2)}, u32[]{:S(2)}) collective-permute-start(f32[160,128]{1,0:T(8,128)S(1)} %get-tuple-element.26), channel_id=1, source_target_pairs={{4,8},{8,4},{5,9},{9,5},{6,10},{10,6},{7,11},{11,7},{20,24},{24,20... | collective-permute-start | bytes 245768 | tf_op jit(solution)/shard_map/ppermute | solution.py:310
  32.7 16.8 %copy-start.1 = (f32[2,16,2048]{2,1,0:T(8,128)S(1)}, f32[2,16,2048]{2,1,0:T(8,128)}, u32[]{:S(2)}) copy-start(f32[2,16,2048]{2,1,0:T(8,128)} %control_ref.1) | copy-start | bytes 786436
  32.7 16.8 %copy-start.9 = (f32[8,8]{1,0:T(8,128)S(1)}, f32[8,8]{1,0:T(8,128)}, u32[]{:S(2)}) copy-start(f32[8,8]{1,0:T(8,128)} %factor_ref.1) | copy-start | bytes 772
  32.7 16.8 %copy-start.11 = (f32[2,8]{1,0:T(2,128)S(1)}, f32[2,8]{1,0:T(2,128)}, u32[]{:S(2)}) copy-start(f32[2,8]{1,0:T(2,128)} %sens_ref.1) | copy-start | bytes 196
  35.9 4.5 %collective-permute-start.9 = (f32[160,128]{1,0:T(8,128)S(1)}, f32[160,128]{1,0:T(8,128)S(1)}, u32[]{:S(2)}, u32[]{:S(2)}) collective-permute-start(f32[160,128]{1,0:T(8,128)S(1)} %get-tuple-element.36), channel_id=1, source_target_pairs={{0,4},{4,0},{8,12},{12,8},{1,5},{5,1},{9,13},{13,9},{2,6},{6,2},{1... | collective-permute-start | bytes 245768 | tf_op jit(solution)/shard_map/ppermute | solution.py:303
  36.0 6.2 %collective-permute-start.10 = (f32[160,128]{1,0:T(8,128)S(1)}, f32[160,128]{1,0:T(8,128)S(1)}, u32[]{:S(2)}, u32[]{:S(2)}) collective-permute-start(f32[160,128]{1,0:T(8,128)S(1)} %get-tuple-element.37), channel_id=1, source_target_pairs={{4,8},{8,4},{5,9},{9,5},{6,10},{10,6},{7,11},{11,7},{20,24},{24,20... | collective-permute-start | bytes 245768 | tf_op jit(solution)/shard_map/ppermute | solution.py:310
  45.1 4.4 %collective-permute-start.11 = (f32[16,2048]{1,0:T(8,128)S(1)}, f32[16,2048]{1,0:T(8,128)S(1)}, u32[]{:S(2)}, u32[]{:S(2)}) collective-permute-start(f32[16,2048]{1,0:T(8,128)S(1)} %shard_map.113.own_ref), channel_id=1, source_target_pairs={{0,1},{1,0},{2,3},{3,2},{4,5},{5,4},{6,7},{7,6},{8,9},{9,8},{10,11... | collective-permute-start | bytes 393224 | tf_op jit(solution)/shard_map/ppermute | solution.py:303

commit v3 on v2

--- a/solution.py
+++ b/solution.py
@@ -104,17 +104,25 @@
     return top, values - top
 
 
-def scatter_kernel(slots, meta_ref, *refs):
-    got_refs, (weight_out, value_out, acc_ref) = refs[:-3], refs[-3:]
+def scatter_kernel(slots, *refs):
+    got_refs, (weight_out, value_out, acc_ref, meta_ref, sems) = refs[:-5], refs[-5:]
+    copies = [
+        pltpu.make_async_copy(got_ref.at[pl.ds(3 * slots, 1)], meta_ref.at[pl.ds(s, 1)], sems.at[s])
+        for s, got_ref in enumerate(got_refs)
+    ]
+    for copy in copies:
+        copy.start()
     rows, width_cols = weight_out.shape
     blocks = width_cols // LANES
     acc_ref[...] = jnp.zeros(acc_ref.shape, F32)
     block_ids = lax.broadcasted_iota(jnp.int32, (blocks, LANES), 0)
     lane_ids = lax.broadcasted_iota(jnp.int32, (LANES, LANES), 0)
     sub = lax.broadcasted_iota(jnp.int32, (GROUP, LANES), 0)
+    for copy in copies:
+        copy.wait()
 
     def source(s, got_ref):
-        count = meta_ref[s, slots]
+        count = meta_ref[s, slots].astype(jnp.int32)
 
         def group(g, carry):
             base = pl.multiple_of(g * GROUP, GROUP)
@@ -134,7 +142,7 @@
                 both = lax.dot_general(
                     left, right, (((1,), (1,)), ((), ())), preferred_element_type=F32
                 )
-                row = meta_ref[s, base + k]
+                row = meta_ref[s, base + k].astype(jnp.int32)
                 at = pl.ds(pl.multiple_of(row * 2 * blocks, 2 * blocks), 2 * blocks)
                 acc_ref[at, :] += both[: 2 * blocks] + both[2 * blocks :]
             return carry
@@ -310,6 +318,10 @@
     return swap(even, "tile", 1), lax.ppermute(odd, "tile", later)
 
 
+def in_hbm(values):
+    return pltpu.with_memory_space_constraint(values, pltpu.HBM)
+
+
 def local(control, diffusivity, land_mask, panel_tile, panel_row, panel_cols, obs_values,
           obs_weights, panel_sensor, sensitivity, cross_factor):
     rows, width = control.shape[1:]
@@ -345,8 +357,8 @@
             pltpu.SemaphoreType.DMA((10,)),
         ],
         cost=cost(4000),
-    )(pos, sensitivity, cross_factor, control, diffusivity, panel_tile.reshape(-1), panel_row,
-      panel_sensor, obs_values, obs_weights, panel_cols)
+    )(pos, *(in_hbm(x) for x in (sensitivity, cross_factor, control, diffusivity, panel_tile.reshape(-1),
+                                 panel_row, panel_sensor, obs_values, obs_weights, panel_cols)))
 
     part = own + swap(other, "var", 1)
     got = [chunks[0]] + [swap(chunks[d], "tile", d) for d in range(1, tiles)]
@@ -363,14 +375,17 @@
     )(pos, part, swap(part, "var", bit))
     even, odd = swap_edges(even, odd)
 
-    meta = jnp.stack([g[3 * slots] for g in got]).astype(jnp.int32)
     weight_sum, value_sum = call(
         functools.partial(scatter_kernel, slots),
         [field, field],
-        [SMEM] + [VMEM] * tiles,
-        [pltpu.VMEM((rows * 2 * blocks, LANES), F32)],
+        [VMEM] * tiles,
+        [
+            pltpu.VMEM((rows * 2 * blocks, LANES), F32),
+            pltpu.SMEM((tiles, LANES), F32),
+            pltpu.SemaphoreType.DMA((tiles,)),
+        ],
         cost=cost(10000),
-    )(meta, *got)
+    )(*got)
 
     ring = pltpu.VMEM((total, width), F32)
     coef, adjoint, even, odd = call(

time: 51.3 us -> 44.8 us (0.87)
  local copies, waits for them, and re-layouts: 7.78 us -> 0.03 us
  starting transfers between devices: 21.3 us -> 16.1 us
  Pallas kernels: 13.7 us -> 17 us
  waiting for transfers between devices: 7.83 us -> 10.8 us
    unnamed x30 -> x10, local copies, waits for them, and re-layouts: 7.77 us -> 0.03 us
    ppermute x3, starting transfers between devices: 12 us -> 5.75 us  [swap_edges(): return (swap(even, 'tile', 1), lax.ppermute(odd, 'tile', later))]
    pallas_call x1, Pallas kernels: 3.1 us -> 6.05 us  [local(): call(functools.partial(scatter_kernel, slots), [field, field], [VMEM] * t...]
    ppermute x9, waiting for transfers between devices: 6.02 us -> 8.61 us  [swap(): return lax.ppermute(values, axis, [(i, i ^ bit) for i in range(count)])]
    ppermute x9, starting transfers between devices: 9.29 us -> 10.3 us  [swap(): return lax.ppermute(values, axis, [(i, i ^ bit) for i in range(count)])]
  transfers between devices with their start and end apart: 12 -> 12, of which waited for: 5 -> 5; matrix products, arithmetic and copies ran while one was open for 0% -> 0% of each run, Pallas kernels for 7% -> 15%
where the time goes in v3:
time: 44.8 us; the launch traced here: 44.2 us
  Pallas kernels  17 us (38%)
  starting transfers between devices  16.1 us (36%)
  waiting for transfers between devices  10.8 us (24%)
    ppermute x9, starting transfers between devices, swap(): return lax.ppermute(values, axis, [(i, i ^ bit) for i in range(count)])  10.3 us
    ppermute x9, waiting for transfers between devices, swap(): return lax.ppermute(values, axis, [(i, i ^ bit) for i in range(count)])  8.61 us
    pallas_call x1, Pallas kernels, local(): call(functools.partial(scatter_kernel, slots), [field, field], [VMEM] * t...  6.05 us
    ppermute x3, starting transfers between devices, swap_edges(): return (swap(even, 'tile', 1), lax.ppermute(odd, 'tile', later))  5.75 us
    pallas_call x1, Pallas kernels, local(): call(functools.partial(analyse_kernel, tiles, margin), [jax.ShapeDtypeStr...  3.22 us
    pallas_call x1, Pallas kernels, local(): call(functools.partial(first_kernel, slots, margin), [field, field, edge2...  2.95 us
    pallas_call x1, Pallas kernels, local(): call(functools.partial(spread_kernel, margin), [field], [SMEM] + [VMEM] *...  2.84 us
    ppermute x3, waiting for transfers between devices, swap_edges(): return (swap(even, 'tile', 1), lax.ppermute(odd, 'tile', later))  2.21 us
  transfers between devices with their start and end apart: 12, of which 5 were waited for; matrix products, arithmetic and copies ran while one was open for 0% of the time, Pallas kernels for 15%

profile of v3, /device:TPU:13, one launch (start us, length us, event | category | flops | bytes accessed | tf_op | source)
XLA Modules:
  0.0 44.2 jit_solution(10755952020603596039)
XLA Ops:
  0.0 0.1 pad_add_fusion.pos_ref
  0.1 2.9 %shard_map.109 = (f32[16,2048]{1,0:T(8,128)S(1)}, f32[16,2048]{1,0:T(8,128)S(1)}, f32[2,160,128]{2,1,0:T(8,128)S(1)}, f32[2,160,128]{2,1,0:T(8,128)S(1)}, f32[20...) custom-call(s32[2]{0:T(128)S(1)} %pad_add_fusion.pos_ref, ...), custom_call_target="tpu_custom_call" | custom-call | flops 16384000 | bytes 4096000 | tf_op jit(solution)/shard_map/pallas_call | solution.py:340
  3.0 0.7 %collective-permute-start = (f32[16,2048]{1,0:T(8,128)S(1)}, f32[16,2048]{1,0:T(8,128)S(1)}, u32[]{:S(2)}, u32[]{:S(2)}) collective-permute-start(f32[16,2048]{1,0:T(8,128)S(1)} %get-tuple-element.23), channel_id=1, source_target_pairs={{0,1},{1,0},{2,3},{3,2},{4,5},{5,4},{6,7},{7,6},{8,9},{9,8},{10,11... | collective-permute-start | bytes 393224 | tf_op jit(solution)/shard_map/ppermute | solution.py:311
  3.8 1.0 %collective-permute-done = f32[16,2048]{1,0:T(8,128)S(1)} collective-permute-done((f32[16,2048]{1,0:T(8,128)S(1)}, f32[16,2048]{1,0:T(8,128)S(1)}, u32[]{:S(2)}, u32[]{:S(2)}) %collective-permute-start) | collective-permute-done | bytes 131104 | tf_op jit(solution)/shard_map/ppermute | solution.py:311
  4.8 1.3 %collective-permute-start.1 = (f32[16,2048]{1,0:T(8,128)S(1)}, f32[16,2048]{1,0:T(8,128)S(1)}, u32[]{:S(2)}, u32[]{:S(2)}) collective-permute-start(f32[16,2048]{1,0:T(8,128)S(1)} %add.3.first_ref), channel_id=1, source_target_pairs={{0,2},{1,3},{2,0},{3,1},{4,6},{5,7},{6,4},{7,5},{8,10},{9,11},{10,... | collective-permute-start | bytes 393224 | tf_op jit(solution)/shard_map/ppermute | solution.py:311
  6.1 0.2 collective-permute-start.6
  6.2 2.3 %collective-permute-start.7 = (f32[200,128]{1,0:T(8,128)S(1)}, f32[200,128]{1,0:T(8,128)S(1)}, u32[]{:S(2)}, u32[]{:S(2)}) collective-permute-start(f32[200,128]{1,0:T(8,128)S(1)} %get-tuple-element.31), channel_id=1, source_target_pairs={{0,8},{4,12},{8,0},{12,4},{1,9},{5,13},{9,1},{13,5},{2,10},{6,14},... | collective-permute-start | bytes 307208 | tf_op jit(solution)/shard_map/ppermute | solution.py:311
  8.5 1.3 %collective-permute-start.4 = (f32[2,160,128]{2,1,0:T(8,128)S(1)}, f32[2,160,128]{2,1,0:T(8,128)S(1)}, u32[]{:S(2)}, u32[]{:S(2)}) collective-permute-start(f32[2,160,128]{2,1,0:T(8,128)S(1)} %get-tuple-element.27), channel_id=1, source_target_pairs={{0,4},{4,0},{8,12},{12,8},{1,5},{5,1},{9,13},{13,9},{2,6},{6,2},{1... | collective-permute-start | bytes 491528 | tf_op jit(solution)/shard_map/ppermute | solution.py:311
  9.8 1.9 %collective-permute-start.5 = (f32[2,160,128]{2,1,0:T(8,128)S(1)}, f32[2,160,128]{2,1,0:T(8,128)S(1)}, u32[]{:S(2)}, u32[]{:S(2)}) collective-permute-start(f32[2,160,128]{2,1,0:T(8,128)S(1)} %get-tuple-element.28), channel_id=1, source_target_pairs={{4,8},{8,4},{5,9},{9,5},{6,10},{10,6},{7,11},{11,7},{20,24},{24,20... | collective-permute-start | bytes 491528 | tf_op jit(solution)/shard_map/ppermute | solution.py:318
  11.8 0.0 collective-permute-done.1.second_ref
  11.8 1.5 %collective-permute-start.8 = (f32[200,128]{1,0:T(8,128)S(1)}, f32[200,128]{1,0:T(8,128)S(1)}, u32[]{:S(2)}, u32[]{:S(2)}) collective-permute-start(f32[200,128]{1,0:T(8,128)S(1)} %get-tuple-element.32), channel_id=1, source_target_pairs={{0,12},{4,8},{8,4},{12,0},{1,13},{5,9},{9,5},{13,1},{2,14},{6,10},... | collective-permute-start | bytes 307208 | tf_op jit(solution)/shard_map/ppermute | solution.py:311
  13.3 0.6 %shard_map.110 = (f32[16,2048]{1,0:T(8,128)S(1)}, f32[160,128]{1,0:T(8,128)S(1)}, f32[160,128]{1,0:T(8,128)S(1)}) custom-call(s32[2]{0:T(128)S(1)} %pad_add_fusion.pos_ref, f32[16,2048]{1,0:T(8,128)S(1)} %add.3.first_ref, f32[16,2048]{1,0:T(8,128)S(1)} %collective-permute-done.1.second_ref), custom_call_target="tpu_custom_call" | custom-call | flops 2048000 | bytes 512000 | tf_op jit(solution)/shard_map/pallas_call | solution.py:370
  13.9 0.0 collective-permute-done.6.refs_1_
  13.9 0.1 collective-permute-start.2
  14.0 0.0 collective-permute-done.7.refs_2_
  14.0 1.9 %collective-permute-start.3 = (f32[160,128]{1,0:T(8,128)S(1)}, f32[160,128]{1,0:T(8,128)S(1)}, u32[]{:S(2)}, u32[]{:S(2)}) collective-permute-start(f32[160,128]{1,0:T(8,128)S(1)} %get-tuple-element.26), channel_id=1, source_target_pairs={{4,8},{8,4},{5,9},{9,5},{6,10},{10,6},{7,11},{11,7},{20,24},{24,20... | collective-permute-start | bytes 245768 | tf_op jit(solution)/shard_map/ppermute | solution.py:318
  15.9 5.3 %collective-permute-done.8.refs_3_ = f32[200,128]{1,0:T(8,128)S(1)} collective-permute-done((f32[200,128]{1,0:T(8,128)S(1)}, f32[200,128]{1,0:T(8,128)S(1)}, u32[]{:S(2)}, u32[]{:S(2)}) %collective-permute-start.8) | collective-permute-done | bytes 102432 | tf_op jit(solution)/shard_map/ppermute | solution.py:311
  21.2 6.1 %shard_map.111 = (f32[16,2048]{1,0:T(8,128)S(1)}, f32[16,2048]{1,0:T(8,128)S(1)}) custom-call(f32[200,128]{1,0:T(8,128)S(1)} %get-tuple-element.29.refs_0_, f32[200,128]{1,0:T(8,128)S(1)} %collective-permute-done.6.refs_1_, f32[200,128]{1,0:T(8,128)S(1)} %collective-permute-done.7.refs_2_, f32[200,128]{1,0:T(8,128)S(1)} %collective-permute-done.8.refs_3_), custom_call_target="tpu_custom_call" | custom-call | flops 40960000 | bytes 10240000 | tf_op jit(solution)/shard_map/pallas_call | solution.py:378
  27.2 0.0 collective-permute-done.4.kappa_even_ref
  27.3 0.0 collective-permute-done.3.odd_ref
  27.3 0.0 copy-start
  27.3 0.0 copy-start.3
  27.3 0.0 copy-start.4
  27.3 3.2 %shard_map.112 = (f32[5,40,2048]{2,1,0:T(8,128)S(1)}, f32[16,2048]{1,0:T(8,128)S(1)}, f32[160,128]{1,0:T(8,128)S(1)}, f32[160,128]{1,0:T(8,128)S(1)}) custom-call(s32[2]{0:T(128)S(1)} %pad_add_fusion.pos_ref, f32[16,2048]{1,0:T(8,128)S(1)} %get-tuple-element.24.own_ref, f32[160,128]{1,0:T(8,128)S(1)} %collective-permute-done.2.even_ref, ...), custom_call_target="tpu_custom_call" | custom-call | flops 20480000 | bytes 5120000 | tf_op jit(solution)/shard_map/pallas_call | solution.py:391
  30.5 0.1 collective-permute-start.9
  30.6 1.9 %collective-permute-start.10 = (f32[160,128]{1,0:T(8,128)S(1)}, f32[160,128]{1,0:T(8,128)S(1)}, u32[]{:S(2)}, u32[]{:S(2)}) collective-permute-start(f32[160,128]{1,0:T(8,128)S(1)} %get-tuple-element.37), channel_id=1, source_target_pairs={{4,8},{8,4},{5,9},{9,5},{6,10},{10,6},{7,11},{11,7},{20,24},{24,20... | collective-permute-start | bytes 245768 | tf_op jit(solution)/shard_map/ppermute | solution.py:318
  32.6 1.3 %collective-permute-done.9.even_ref = f32[160,128]{1,0:T(8,128)S(1)} collective-permute-done((f32[160,128]{1,0:T(8,128)S(1)}, f32[160,128]{1,0:T(8,128)S(1)}, u32[]{:S(2)}, u32[]{:S(2)}) %collective-permute-start.9) | collective-permute-done | bytes 81952 | tf_op jit(solution)/shard_map/ppermute | solution.py:311
  33.9 2.2 %collective-permute-done.10.odd_ref = f32[160,128]{1,0:T(8,128)S(1)} collective-permute-done((f32[160,128]{1,0:T(8,128)S(1)}, f32[160,128]{1,0:T(8,128)S(1)}, u32[]{:S(2)}, u32[]{:S(2)}) %collective-permute-start.10) | collective-permute-done | bytes 81952 | tf_op jit(solution)/shard_map/ppermute | solution.py:318
  36.1 2.8 %shard_map.113.own_ref = f32[16,2048]{1,0:T(8,128)S(1)} custom-call(s32[2]{0:T(128)S(1)} %pad_add_fusion.pos_ref, f32[16,2048]{1,0:T(8,128)S(1)} %get-tuple-element.35.own_ref, f32[160,128]{1,0:T(8,128)S(1)} %collective-permute-done.9.even_ref, f32[160,128]{1,0:T(8,128)S(1)} %collective-permute-done.10.odd_ref, f32[5,40,2048]{2,1,0:T(8,128)S(1)} %get-tuple-element.38.coef_ref), custom_call_target="tpu_custom_call" | custom-call | flops 16384000 | bytes 4096000 | tf_op jit(solution)/shard_map/pallas_call | solution.py:399
  39.0 2.9 %collective-permute-start.11 = (f32[16,2048]{1,0:T(8,128)S(1)}, f32[16,2048]{1,0:T(8,128)S(1)}, u32[]{:S(2)}, u32[]{:S(2)}) collective-permute-start(f32[16,2048]{1,0:T(8,128)S(1)} %shard_map.113.own_ref), channel_id=1, source_target_pairs={{0,1},{1,0},{2,3},{3,2},{4,5},{5,4},{6,7},{7,6},{8,9},{9,8},{10,11... | collective-permute-start | bytes 393224 | tf_op jit(solution)/shard_map/ppermute | solution.py:311
  41.8 1.0 %collective-permute-done.11.other_ref = f32[16,2048]{1,0:T(8,128)S(1)} collective-permute-done((f32[16,2048]{1,0:T(8,128)S(1)}, f32[16,2048]{1,0:T(8,128)S(1)}, u32[]{:S(2)}, u32[]{:S(2)}) %collective-permute-start.11) | collective-permute-done | bytes 131104 | tf_op jit(solution)/shard_map/ppermute | solution.py:311
  42.8 1.4 %shard_map.114 = f32[2,16,2048]{2,1,0:T(8,128)} custom-call(s32[2]{0:T(128)S(1)} %pad_add_fusion.pos_ref, f32[2,8]{1,0:T(2,128)S(1)} %copy-done.4, f32[8,8]{1,0:T(8,128)S(1)} %copy-done.3, f32[2,16,2048]{2,1,0:T(8,128)S(1)} %copy-done, f32[16,2048]{1,0:T(8,128)S(1)} %shard_map.113.own_ref, f32[16,2048]{1,0:T(8,128)S(1)} %collective-permute-done.11.other_ref), custom_call_target="tpu_custom_call" | custom-call | flops 4096000 | bytes 1024000 | tf_op jit(solution)/shard_map/pallas_call | solution.py:406
  (10 shorter events, 0.0 us)
Async XLA Ops:
  0.0 27.3 %copy-start.1 = (f32[2,16,2048]{2,1,0:T(8,128)S(1)}, f32[2,16,2048]{2,1,0:T(8,128)}, u32[]{:S(2)}) copy-start(f32[2,16,2048]{2,1,0:T(8,128)} %kappa_ref.1) | copy-start | bytes 786436
  0.0 27.3 %copy-start.2 = (s32[16,2048]{1,0:T(8,128)S(1)}, s32[16,2048]{1,0:T(8,128)}, u32[]{:S(2)}) copy-start(s32[16,2048]{1,0:T(8,128)} %mask_ref.1) | copy-start | bytes 393220
  3.0 1.7 %collective-permute-start = (f32[16,2048]{1,0:T(8,128)S(1)}, f32[16,2048]{1,0:T(8,128)S(1)}, u32[]{:S(2)}, u32[]{:S(2)}) collective-permute-start(f32[16,2048]{1,0:T(8,128)S(1)} %get-tuple-element.23), channel_id=1, source_target_pairs={{0,1},{1,0},{2,3},{3,2},{4,5},{5,4},{6,7},{7,6},{8,9},{9,8},{10,11... | collective-permute-start | bytes 393224 | tf_op jit(solution)/shard_map/ppermute | solution.py:311
  4.8 7.0 %collective-permute-start.1 = (f32[16,2048]{1,0:T(8,128)S(1)}, f32[16,2048]{1,0:T(8,128)S(1)}, u32[]{:S(2)}, u32[]{:S(2)}) collective-permute-start(f32[16,2048]{1,0:T(8,128)S(1)} %add.3.first_ref), channel_id=1, source_target_pairs={{0,2},{1,3},{2,0},{3,1},{4,6},{5,7},{6,4},{7,5},{8,10},{9,11},{10,... | collective-permute-start | bytes 393224 | tf_op jit(solution)/shard_map/ppermute | solution.py:311
  6.1 7.8 %collective-permute-start.6 = (f32[200,128]{1,0:T(8,128)S(1)}, f32[200,128]{1,0:T(8,128)S(1)}, u32[]{:S(2)}, u32[]{:S(2)}) collective-permute-start(f32[200,128]{1,0:T(8,128)S(1)} %get-tuple-element.30), channel_id=1, source_target_pairs={{0,4},{4,0},{8,12},{12,8},{1,5},{5,1},{9,13},{13,9},{2,6},{6,2},{1... | collective-permute-start | bytes 307208 | tf_op jit(solution)/shard_map/ppermute | solution.py:311
  6.2 7.7 %collective-permute-start.7 = (f32[200,128]{1,0:T(8,128)S(1)}, f32[200,128]{1,0:T(8,128)S(1)}, u32[]{:S(2)}, u32[]{:S(2)}) collective-permute-start(f32[200,128]{1,0:T(8,128)S(1)} %get-tuple-element.31), channel_id=1, source_target_pairs={{0,8},{4,12},{8,0},{12,4},{1,9},{5,13},{9,1},{13,5},{2,10},{6,14},... | collective-permute-start | bytes 307208 | tf_op jit(solution)/shard_map/ppermute | solution.py:311
  8.5 18.7 %collective-permute-start.4 = (f32[2,160,128]{2,1,0:T(8,128)S(1)}, f32[2,160,128]{2,1,0:T(8,128)S(1)}, u32[]{:S(2)}, u32[]{:S(2)}) collective-permute-start(f32[2,160,128]{2,1,0:T(8,128)S(1)} %get-tuple-element.27), channel_id=1, source_target_pairs={{0,4},{4,0},{8,12},{12,8},{1,5},{5,1},{9,13},{13,9},{2,6},{6,2},{1... | collective-permute-start | bytes 491528 | tf_op jit(solution)/shard_map/ppermute | solution.py:311
  9.8 17.4 %collective-permute-start.5 = (f32[2,160,128]{2,1,0:T(8,128)S(1)}, f32[2,160,128]{2,1,0:T(8,128)S(1)}, u32[]{:S(2)}, u32[]{:S(2)}) collective-permute-start(f32[2,160,128]{2,1,0:T(8,128)S(1)} %get-tuple-element.28), channel_id=1, source_target_pairs={{4,8},{8,4},{5,9},{9,5},{6,10},{10,6},{7,11},{11,7},{20,24},{24,20... | collective-permute-start | bytes 491528 | tf_op jit(solution)/shard_map/ppermute | solution.py:318
  11.8 9.4 %collective-permute-start.8 = (f32[200,128]{1,0:T(8,128)S(1)}, f32[200,128]{1,0:T(8,128)S(1)}, u32[]{:S(2)}, u32[]{:S(2)}) collective-permute-start(f32[200,128]{1,0:T(8,128)S(1)} %get-tuple-element.32), channel_id=1, source_target_pairs={{0,12},{4,8},{8,4},{12,0},{1,13},{5,9},{9,5},{13,1},{2,14},{6,10},... | collective-permute-start | bytes 307208 | tf_op jit(solution)/shard_map/ppermute | solution.py:311
  13.9 13.4 %collective-permute-start.2 = (f32[160,128]{1,0:T(8,128)S(1)}, f32[160,128]{1,0:T(8,128)S(1)}, u32[]{:S(2)}, u32[]{:S(2)}) collective-permute-start(f32[160,128]{1,0:T(8,128)S(1)} %get-tuple-element.25), channel_id=1, source_target_pairs={{0,4},{4,0},{8,12},{12,8},{1,5},{5,1},{9,13},{13,9},{2,6},{6,2},{1... | collective-permute-start | bytes 245768 | tf_op jit(solution)/shard_map/ppermute | solution.py:311
  14.0 13.3 %collective-permute-start.3 = (f32[160,128]{1,0:T(8,128)S(1)}, f32[160,128]{1,0:T(8,128)S(1)}, u32[]{:S(2)}, u32[]{:S(2)}) collective-permute-start(f32[160,128]{1,0:T(8,128)S(1)} %get-tuple-element.26), channel_id=1, source_target_pairs={{4,8},{8,4},{5,9},{9,5},{6,10},{10,6},{7,11},{11,7},{20,24},{24,20... | collective-permute-start | bytes 245768 | tf_op jit(solution)/shard_map/ppermute | solution.py:318
  27.3 15.5 %copy-start = (f32[2,16,2048]{2,1,0:T(8,128)S(1)}, f32[2,16,2048]{2,1,0:T(8,128)}, u32[]{:S(2)}) copy-start(f32[2,16,2048]{2,1,0:T(8,128)} %control_ref.1) | copy-start | bytes 786436
  27.3 15.5 %copy-start.3 = (f32[8,8]{1,0:T(8,128)S(1)}, f32[8,8]{1,0:T(8,128)}, u32[]{:S(2)}) copy-start(f32[8,8]{1,0:T(8,128)} %factor_ref.1) | copy-start | bytes 772
  27.3 15.5 %copy-start.4 = (f32[2,8]{1,0:T(2,128)S(1)}, f32[2,8]{1,0:T(2,128)}, u32[]{:S(2)}) copy-start(f32[2,8]{1,0:T(2,128)} %sens_ref.1) | copy-start | bytes 196
  30.5 3.4 %collective-permute-start.9 = (f32[160,128]{1,0:T(8,128)S(1)}, f32[160,128]{1,0:T(8,128)S(1)}, u32[]{:S(2)}, u32[]{:S(2)}) collective-permute-start(f32[160,128]{1,0:T(8,128)S(1)} %get-tuple-element.36), channel_id=1, source_target_pairs={{0,4},{4,0},{8,12},{12,8},{1,5},{5,1},{9,13},{13,9},{2,6},{6,2},{1... | collective-permute-start | bytes 245768 | tf_op jit(solution)/shard_map/ppermute | solution.py:311
  30.6 5.5 %collective-permute-start.10 = (f32[160,128]{1,0:T(8,128)S(1)}, f32[160,128]{1,0:T(8,128)S(1)}, u32[]{:S(2)}, u32[]{:S(2)}) collective-permute-start(f32[160,128]{1,0:T(8,128)S(1)} %get-tuple-element.37), channel_id=1, source_target_pairs={{4,8},{8,4},{5,9},{9,5},{6,10},{10,6},{7,11},{11,7},{20,24},{24,20... | collective-permute-start | bytes 245768 | tf_op jit(solution)/shard_map/ppermute | solution.py:318
  39.0 3.9 %collective-permute-start.11 = (f32[16,2048]{1,0:T(8,128)S(1)}, f32[16,2048]{1,0:T(8,128)S(1)}, u32[]{:S(2)}, u32[]{:S(2)}) collective-permute-start(f32[16,2048]{1,0:T(8,128)S(1)} %shard_map.113.own_ref), channel_id=1, source_target_pairs={{0,1},{1,0},{2,3},{3,2},{4,5},{5,4},{6,7},{7,6},{8,9},{9,8},{10,11... | collective-permute-start | bytes 393224 | tf_op jit(solution)/shard_map/ppermute | solution.py:311
